TPU v7x, 256 devices: a whole 4x4x8 slice. The times are simulated.
256 devices in a mesh: grp: 8 (over z), dom: 32 (over x, y, core).
Axes of the slice: x: 4, y: 4, z: 8, core: 2. Of those that a mesh axis runs over, the one named last changes fastest.
Arguments:
- right_side: float32 [8, 32, 5, 2048], P('grp', 'dom'), may hold values from -6 to 6
- initial_guess: float32 [8, 32, 5, 2048], P('grp', 'dom'), may hold values from -3 to 3
- fine_diag: float32 [8, 32, 5, 5, 2048], P('grp', 'dom')
- fine_inverse: float32 [8, 32, 5, 5, 2048], P('grp', 'dom')
- fine_coupling: float32 [8, 32, 6, 5, 5, 2048], P('grp', 'dom'), may hold values from -1.4 to 1.4
- fine_columns: int32 [8, 32, 6, 2048], P('grp', 'dom'), may hold values from 0 to 2303, as said below
- fine_send: int32 [8, 32, 4, 64], P('grp', 'dom'), may hold values from 0 to 2047
- fine_count: int32 [8, 32, 4], P('grp', 'dom'), may hold values from 16 to 64, as said below
- fine_aggregate: int32 [8, 32, 2048], P('grp', 'dom'), may hold values from 0 to 511, as said below
- middle_diag: float32 [8, 32, 5, 5, 512], P('grp', 'dom')
- middle_inverse: float32 [8, 32, 5, 5, 512], P('grp', 'dom')
- middle_coupling: float32 [8, 32, 6, 5, 5, 512], P('grp', 'dom'), may hold values from -1.4 to 1.4
- middle_columns: int32 [8, 32, 6, 512], P('grp', 'dom'), may hold values from 0 to 1087
- middle_aggregate: int32 [8, 32, 512], P('grp', 'dom'), may hold values from 0 to 127, as said below
- coarse_diag: float32 [8, 32, 5, 5, 128], P('grp', 'dom')
- coarse_inverse: float32 [8, 32, 5, 5, 128], P('grp', 'dom')
- coarse_coupling: float32 [8, 32, 6, 5, 5, 128], P('grp', 'dom'), may hold values from -1.4 to 1.4
- coarse_columns: int32 [8, 32, 6, 128], P('grp', 'dom'), may hold values from 0 to 511
Outputs:
- solution: float32 [8, 32, 5, 2048], P('grp', 'dom')
Inputs may be any that keep to these rules, and one draw needn't show every extreme that they name: `fine_count`: at least one of the four counts of each device is 64; the others are ragged. `fine_columns`: columns below 2048 are own rows; a column 2048 + j * 64 + s names slot s of the j-th received block, with s below the sender's count. `fine_aggregate`: each middle row gathers exactly four fine rows of its device. `middle_aggregate`: each coarse row gathers exactly four middle rows of its device.
All inputs are finite; a program needn't handle non-finite values.
Results may differ from a plain program's by a relative error of at most 0.0003.
Values sent between devices are 32-bit elements; how exact they have to be, the bound alone decides.
No kernel may reach another device: no remote copies, remote signals or barrier semaphores. Data moves between devices by JAX's collectives and lax.ppermute only.
A program may use at most 128 MiB of HBM per device.

v0:
```python
import functools

import jax
import jax.numpy as jnp
from jax import lax
from jax.experimental import pallas as pl
from jax.experimental.pallas import tpu as pltpu
from jax.sharding import PartitionSpec as P

ROWS_FINE = 2048
ROWS_MID = 512
ROWS_COARSE = 128
SLOT_ROWS = 64
RIM_ROWS = 32
LANES = 128
OFFSETS = (-2, -1, 1, 2)
RELAX = 0.8
F32 = jnp.float32


def lane_pick(chunk, index):
    return jnp.take_along_axis(chunk, index, axis=1, mode="promise_in_bounds")


def pick(table, index_row, chunks):
    index = jnp.broadcast_to(index_row, (8, LANES))
    low = index & (LANES - 1)
    level = [lane_pick(table(t), low) for t in range(chunks)]
    bit = 0
    while len(level) > 1:
        odd = (index & (LANES << bit)) != 0
        level = [
            jnp.where(odd, level[i + 1], level[i]) if i + 1 < len(level) else level[i]
            for i in range(0, len(level), 2)
        ]
        bit += 1
    return level[0]


def padded(value):
    return jnp.concatenate([value, jnp.zeros((3, value.shape[1]), value.dtype)], axis=0)


def rows_of(parts):
    return jnp.concatenate([jnp.sum(part, axis=0, keepdims=True) for part in parts], axis=0)


def apply_chunk(diag, coupling, columns, table, chunks, rows, remap=None):
    own = table(None)
    parts = [diag[i, :, rows] * own for i in range(5)]
    for n in range(6):
        index = columns[n : n + 1, rows]
        if remap is not None:
            index = remap(index)
        picked = pick(table, index, chunks)[:5]
        for i in range(5):
            parts[i] = parts[i] + coupling[n, i, :, rows] * picked
    return rows_of(parts)


def inverse_chunk(inverse, value, rows):
    return rows_of([inverse[i, :, rows] * value for i in range(5)])


def lane_slice(c):
    return pl.ds(pl.multiple_of(c * LANES, LANES), LANES)


def split3(value):
    first = value.astype(jnp.bfloat16)
    rest = value - first.astype(F32)
    second = rest.astype(jnp.bfloat16)
    third = (rest - second.astype(F32)).astype(jnp.bfloat16)
    return first, second, third


def restrict(residual, aggregate, number, store):
    rows = aggregate.shape[1]
    groups = number // LANES
    total = jnp.zeros((3 * 8 * groups, LANES), F32)
    step = min(rows, 512)
    for start in range(0, rows, step):
        index = aggregate[:, start : start + step]
        value = residual(start, step)
        high = index >> 7
        low = index & (LANES - 1)
        left = []
        for piece in split3(value):
            wide = piece.astype(F32)
            left += [jnp.where(high == h, wide, 0.0) for h in range(groups)]
        left = jnp.concatenate(left, axis=0).astype(jnp.bfloat16)
        lanes = lax.broadcasted_iota(jnp.int32, (LANES, step), 0)
        hot = jnp.where(lanes == low, 1.0, 0.0).astype(jnp.bfloat16)
        total = total + lax.dot_general(
            left, hot, (((1,), (1,)), ((), ())), preferred_element_type=F32
        )
    size = 8 * groups
    summed = total[:size] + total[size : 2 * size] + total[2 * size :]
    for h in range(groups):
        store(h, summed[h * 8 : h * 8 + 8])


def load_fine(x, received, ext):
    for c in range(ROWS_FINE // LANES):
        ext[c, 0:5] = x[:, c * LANES : (c + 1) * LANES]
    for j in range(4):
        lane = (j % 2) * SLOT_ROWS
        ext[16 + j // 2, 0:5, lane : lane + SLOT_ROWS] = received[j][...]


def pack_sends(table, send, count, outs):
    position = lax.broadcasted_iota(jnp.int32, (1, SLOT_ROWS), 1)
    for pair in range(2):
        index = jnp.concatenate([send[2 * pair : 2 * pair + 1], send[2 * pair + 1 : 2 * pair + 2]], axis=1)
        picked = pick(table, index, 16)[:5]
        for half in range(2):
            j = 2 * pair + half
            live = (position < count[j]).astype(F32)
            outs[j][...] = picked[:, half * SLOT_ROWS : (half + 1) * SLOT_ROWS] * live


def send_kernel(x, send, count, s0, s1, s2, s3):
    pack_sends(
        lambda t: padded(x[:, t * LANES : (t + 1) * LANES]), send, count, (s0, s1, s2, s3)
    )


def fine_sweep_body(x, b, diag, inverse, coupling, columns, ext, result):
    def body(c, carry):
        rows = lane_slice(c)
        own = ext[c][:5]
        table = lambda t: own if t is None else ext[t]
        image = apply_chunk(diag, coupling, columns, table, 18, rows)
        change = inverse_chunk(inverse, b[:, rows] - image, rows)
        result(c, own + RELAX * change)
        return carry

    lax.fori_loop(0, 16, body, 0, unroll=4)


def fine_kernel(last, x, b, diag, inverse, coupling, columns, send, count, r3, r2, r1, r0, *rest):
    if last:
        new, ext = rest
        outs = None
    else:
        new, s0, s1, s2, s3, ext, fresh = rest
        outs = (s0, s1, s2, s3)
    load_fine(x, (r0, r1, r2, r3), ext)

    def result(c, value):
        new[:, lane_slice(c)] = value
        if not last:
            fresh[c, 0:5] = value

    fine_sweep_body(x, b, diag, inverse, coupling, columns, ext, result)
    if not last:
        pack_sends(lambda t: fresh[t], send, count, outs)


def down_kernel(
    x, b, diag, coupling, columns, aggregate, m_inverse, r3, r2, r1, r0, rhs, e, ext, residual
):
    load_fine(x, (r0, r1, r2, r3), ext)
    residual[5:8, :] = jnp.zeros((3, ROWS_FINE), F32)

    def body(c, carry):
        rows = lane_slice(c)
        own = ext[c][:5]
        table = lambda t: own if t is None else ext[t]
        image = apply_chunk(diag, coupling, columns, table, 18, rows)
        residual[0:5, rows] = b[:, rows] - image
        return carry

    lax.fori_loop(0, 16, body, 0, unroll=4)

    def store(h, value):
        rows = slice(h * LANES, (h + 1) * LANES)
        rhs[:, rows] = value[:5]
        e[:, rows] = RELAX * inverse_chunk(m_inverse, value[:5], rows)

    restrict(lambda s, n: residual[:, s : s + n], aggregate, ROWS_MID, store)


def middle_remap(index):
    own = index - RIM_ROWS
    left = index + 2 * ROWS_MID
    right = index + ROWS_MID
    partner = index - 2 * RIM_ROWS
    return jnp.where(
        index < RIM_ROWS,
        left,
        jnp.where(
            index < RIM_ROWS + ROWS_MID,
            own,
            jnp.where(index < 2 * RIM_ROWS + ROWS_MID, right, partner),
        ),
    )


def load_middle(e, left, right, partner, ext):
    for c in range(4):
        ext[c, 0:5] = e[:, c * LANES : (c + 1) * LANES]
        ext[4 + c, 0:5] = partner[:, c * LANES : (c + 1) * LANES]
    ext[8, 0:5, 0:RIM_ROWS] = left[:, ROWS_MID - RIM_ROWS : ROWS_MID]
    ext[8, 0:5, RIM_ROWS : 2 * RIM_ROWS] = right[:, 0:RIM_ROWS]


def middle_rows(e_table, c, diag, coupling, columns):
    rows = slice(c * LANES, (c + 1) * LANES)
    own = e_table[c][:5]
    table = lambda t: own if t is None else e_table[t]
    return rows, own, apply_chunk(diag, coupling, columns, table, 9, rows, middle_remap)


def middle_kernel(e, rhs, diag, inverse, coupling, columns, right, left, partner, new, ext):
    load_middle(e, left, right, partner, ext)
    for c in range(4):
        rows, own, image = middle_rows(ext, c, diag, coupling, columns)
        new[:, rows] = own + RELAX * inverse_chunk(inverse, rhs[:, rows] - image, rows)


def coarse_down_kernel(
    e, rhs, diag, coupling, columns, right, left, partner, aggregate, c_inverse, c_rhs, c_new, ext, residual
):
    load_middle(e, left, right, partner, ext)
    residual[5:8, :] = jnp.zeros((3, ROWS_MID), F32)
    for c in range(4):
        rows, own, image = middle_rows(ext, c, diag, coupling, columns)
        residual[0:5, rows] = rhs[:, rows] - image

    def store(h, value):
        rows = slice(0, LANES)
        c_rhs[...] = value[:5]
        c_new[...] = RELAX * inverse_chunk(c_inverse, value[:5], rows)

    restrict(lambda s, n: residual[:, s : s + n], aggregate, ROWS_COARSE, store)


def coarse_rows(c_field, others, diag, inverse, coupling, columns, rhs):
    rows = slice(0, LANES)
    members = [padded(r[...]) for r in (c_field,) + others]
    own = c_field[...]
    table = lambda t: own if t is None else members[t]
    image = apply_chunk(diag, coupling, columns, table, 4, rows)
    return own + RELAX * inverse_chunk(inverse, rhs[...] - image, rows)


def coarse_kernel(field, rhs, diag, inverse, coupling, columns, p3, p2, p1, new):
    new[...] = coarse_rows(field, (p1, p2, p3), diag, inverse, coupling, columns, rhs)


def coarse_up_kernel(field, rhs, diag, inverse, coupling, columns, p3, p2, p1, e, aggregate, new):
    done = padded(coarse_rows(field, (p1, p2, p3), diag, inverse, coupling, columns, rhs))
    for c in range(4):
        rows = slice(c * LANES, (c + 1) * LANES)
        new[:, rows] = e[:, rows] + pick(lambda t: done, aggregate[:, rows], 1)[:5]


def middle_up_kernel(
    e, rhs, diag, inverse, coupling, columns, right, left, partner, x, aggregate, send, count,
    new, s0, s1, s2, s3, ext, done, fresh
):
    load_middle(e, left, right, partner, ext)
    for c in range(4):
        rows, own, image = middle_rows(ext, c, diag, coupling, columns)
        done[c, 0:5] = own + RELAX * inverse_chunk(inverse, rhs[:, rows] - image, rows)
    for c in range(16):
        rows = slice(c * LANES, (c + 1) * LANES)
        value = x[:, rows] + pick(lambda t: done[t], aggregate[:, rows], 4)[:5]
        new[:, rows] = value
        fresh[c, 0:5] = value
    pack_sends(lambda t: fresh[t], send, count, (s0, s1, s2, s3))


VMEM = pl.BlockSpec(memory_space=pltpu.VMEM)
SMEM = pl.BlockSpec(memory_space=pltpu.SMEM)


def call(name, kernel, args, shapes, scratch=(), scalars=()):
    return pl.pallas_call(
        kernel,
        name=name,
        out_shape=[jax.ShapeDtypeStruct(s, F32) for s in shapes],
        in_specs=[SMEM if i in scalars else VMEM for i in range(len(args))],
        out_specs=[VMEM] * len(shapes),
        scratch_shapes=[pltpu.VMEM(s, F32) for s in scratch],
        compiler_params=pltpu.CompilerParams(vmem_limit_bytes=16 * 1024 * 1024),
    )(*args)


def passed_along(x, by):
    size = lax.axis_size("dom")
    return lax.ppermute(x, "dom", [(i, (i + by) % size) for i in range(size)])


def group_swap(x, mask):
    return lax.ppermute(x, "grp", [(i, i ^ mask) for i in range(lax.axis_size("grp"))])


def per_device(
    right_side, initial_guess, fine_diag, fine_inverse, fine_coupling, fine_columns, fine_send, fine_count,
    fine_aggregate, middle_diag, middle_inverse, middle_coupling, middle_columns, middle_aggregate,
    coarse_diag, coarse_inverse, coarse_coupling, coarse_columns,
):
    b, x = right_side[0, 0], initial_guess[0, 0]
    f_mats = (fine_diag[0, 0], fine_inverse[0, 0], fine_coupling[0, 0], fine_columns[0, 0])
    f_send, f_count, f_aggregate = fine_send[0, 0], fine_count[0, 0], fine_aggregate[0]
    m_mats = (middle_diag[0, 0], middle_inverse[0, 0], middle_coupling[0, 0], middle_columns[0, 0])
    m_aggregate = middle_aggregate[0]
    c_mats = (coarse_diag[0, 0], coarse_inverse[0, 0], coarse_coupling[0, 0], coarse_columns[0, 0])

    slot = (5, SLOT_ROWS)
    fine = (5, ROWS_FINE)
    mid = (5, ROWS_MID)
    coarse = (5, ROWS_COARSE)
    f_ext, f_fresh = (18, 8, LANES), (16, 8, LANES)
    m_ext = (9, 8, LANES)

    def fine_exchange(sends):
        received = [passed_along(sends[3 - j], -OFFSETS[j]) for j in (3, 2, 1, 0)]
        return received

    def middle_exchange(e):
        right = passed_along(e, -1)
        left = passed_along(e, 1)
        return [right, left, group_swap(e, 1)]

    def coarse_exchange(c):
        return [group_swap(c, mask) for mask in (3, 2, 1)]

    def fine_sweep(name, x, sends, last=False):
        received = fine_exchange(sends)
        out = call(
            name,
            functools.partial(fine_kernel, last),
            (x, b) + f_mats + (f_send, f_count, *received),
            [fine] if last else [fine] + [slot] * 4,
            [f_ext] if last else [f_ext, f_fresh],
            scalars=(7,),
        )
        return out[0], out[1:]

    sends = call("send", send_kernel, (x, f_send, f_count), [slot] * 4, scalars=(2,))
    x, sends = fine_sweep("fine_1", x, sends)
    x, sends = fine_sweep("fine_2", x, sends)
    rhs, e = call(
        "down",
        down_kernel,
        (x, b, f_mats[0], f_mats[2], f_mats[3], f_aggregate, m_mats[1], *fine_exchange(sends)),
        [mid, mid],
        [f_ext, (8, ROWS_FINE)],
    )

    def middle_sweep(name, e):
        return call(
            name, middle_kernel, (e, rhs) + m_mats + tuple(middle_exchange(e)),
            [mid], [m_ext],
        )

    (e,) = middle_sweep("middle_2", e)
    c_rhs, c = call(
        "coarse_down",
        coarse_down_kernel,
        (e, rhs, m_mats[0], m_mats[2], m_mats[3], *middle_exchange(e), m_aggregate, c_mats[1]),
        [coarse, coarse],
        [m_ext, (8, ROWS_MID)],
    )
    (c,) = call("coarse_2", coarse_kernel, (c, c_rhs) + c_mats + tuple(coarse_exchange(c)), [coarse])
    (e,) = call(
        "coarse_3",
        coarse_up_kernel,
        (c, c_rhs) + c_mats + tuple(coarse_exchange(c)) + (e, m_aggregate),
        [mid],
    )
    (e,) = middle_sweep("middle_3", e)
    out = call(
        "middle_4",
        middle_up_kernel,
        (e, rhs) + m_mats + tuple(middle_exchange(e)) + (x, f_aggregate, f_send, f_count),
        [fine] + [slot] * 4,
        [m_ext, (4, 8, LANES), f_fresh],
        scalars=(12,),
    )
    x, sends = out[0], out[1:]
    x, sends = fine_sweep("fine_4", x, sends)
    x, _ = fine_sweep("fine_5", x, sends, last=True)
    return x[None, None]


def solution(mesh):
    def spec(rank):
        return P("grp", "dom", *([None] * (rank - 2)))

    ranks = (4, 4, 5, 5, 6, 4, 4, 3, 3, 5, 5, 6, 4, 3, 5, 5, 6, 4)
    return jax.shard_map(
        per_device,
        mesh=mesh,
        in_specs=tuple(spec(rank) for rank in ranks),
        out_specs=spec(4),
        check_vma=False,
    )
```

profile of v0, /device:TPU:1, one launch (start us, length us, event | category | flops | bytes accessed | tf_op | source)
XLA Modules:
  0.0 119.9 jit_solution(10999484743028955066)
XLA Ops:
  2.9 5.8 %collective-permute-start = (f32[5,64]{1,0:T(8,128)S(1)}, f32[5,64]{1,0:T(8,128)S(1)}, u32[]{:S(2)}, u32[]{:S(2)}) collective-permute-start(f32[5,64]{1,0:T(8,128)S(1)} %get-tuple-element.33), channel_id=1, source_target_pairs={{0,30},{1,31},{2,0},{3,1},{4,2},{5,3},{6,4},{7,5},{8,6},{9,7},{10,... | collective-permute-start | bytes 3848 | tf_op jit(solution)/shard_map/ppermute | solution.py:293
  11.7 1.9 %copy.63 = f32[1,1,6,5,5,2048]{5,4,3,2,0,1:T(8,128)S(1)} copy(f32[1,1,6,5,5,2048]{5,1,4,3,2,0:T(1,128)} %param.22) | data formatting | bytes 2457600 | tf_op jit(solution)/shard_map/squeeze | solution.py:306
  13.6 2.6 %collective-permute-done.3.r0 = f32[5,64]{1,0:T(8,128)S(1)} collective-permute-done((f32[5,64]{1,0:T(8,128)S(1)}, f32[5,64]{1,0:T(8,128)S(1)}, u32[]{:S(2)}, u32[]{:S(2)}) %collective-permute-start.3) | collective-permute-done | bytes 1312 | tf_op jit(solution)/shard_map/ppermute | solution.py:293
  16.2 3.4 %fine_1.1 = (f32[5,2048]{1,0:T(8,128)S(1)}, f32[5,64]{1,0:T(8,128)S(1)}, f32[5,64]{1,0:T(8,128)S(1)}, f32[5,64]{1,0:T(8,128)S(1)}, f32[5,64]{1,0:T(8,128)S(1)}) custom-call(f32[5,2048]{1,0:T(8,128)S(1)} %bitcast.78, f32[5,2048]{1,0:T(8,128)S(1)} %bitcast.62, f32[5,5,2048]{2,1,0:T(8,128)S(1)} %get-tuple-element.62.diag, ...), custom_call_target="tpu_custom_call" | custom-call | tf_op jit(solution)/shard_map/fine_1/pallas_call | solution.py:280
  19.6 2.3 %collective-permute-start.4 = (f32[5,64]{1,0:T(8,128)S(1)}, f32[5,64]{1,0:T(8,128)S(1)}, u32[]{:S(2)}, u32[]{:S(2)}) collective-permute-start(f32[5,64]{1,0:T(8,128)S(1)} %get-tuple-element.38), channel_id=1, source_target_pairs={{0,30},{1,31},{2,0},{3,1},{4,2},{5,3},{6,4},{7,5},{8,6},{9,7},{10,... | collective-permute-start | bytes 3848 | tf_op jit(solution)/shard_map/ppermute | solution.py:293
  24.9 4.5 %collective-permute-done.7.r0 = f32[5,64]{1,0:T(8,128)S(1)} collective-permute-done((f32[5,64]{1,0:T(8,128)S(1)}, f32[5,64]{1,0:T(8,128)S(1)}, u32[]{:S(2)}, u32[]{:S(2)}) %collective-permute-start.7) | collective-permute-done | bytes 1312 | tf_op jit(solution)/shard_map/ppermute | solution.py:293
  29.4 3.4 %fine_2.1 = (f32[5,2048]{1,0:T(8,128)S(1)}, f32[5,64]{1,0:T(8,128)S(1)}, f32[5,64]{1,0:T(8,128)S(1)}, f32[5,64]{1,0:T(8,128)S(1)}, f32[5,64]{1,0:T(8,128)S(1)}) custom-call(f32[5,2048]{1,0:T(8,128)S(1)} %get-tuple-element.37.x, f32[5,2048]{1,0:T(8,128)S(1)} %bitcast.63, f32[5,5,2048]{2,1,0:T(8,128)S(1)} %get-tuple-element.62.diag, ...), custom_call_target="tpu_custom_call" | custom-call | tf_op jit(solution)/shard_map/fine_2/pallas_call | solution.py:280
  33.0 5.0 %collective-permute-start.8 = (f32[5,64]{1,0:T(8,128)S(1)}, f32[5,64]{1,0:T(8,128)S(1)}, u32[]{:S(2)}, u32[]{:S(2)}) collective-permute-start(f32[5,64]{1,0:T(8,128)S(1)} %get-tuple-element.43), channel_id=1, source_target_pairs={{0,30},{1,31},{2,0},{3,1},{4,2},{5,3},{6,4},{7,5},{8,6},{9,7},{10,... | collective-permute-start | bytes 3848 | tf_op jit(solution)/shard_map/ppermute | solution.py:293
  39.2 1.7 %collective-permute-done.9.r2 = f32[5,64]{1,0:T(8,128)S(1)} collective-permute-done((f32[5,64]{1,0:T(8,128)S(1)}, f32[5,64]{1,0:T(8,128)S(1)}, u32[]{:S(2)}, u32[]{:S(2)}) %collective-permute-start.9) | collective-permute-done | bytes 1312 | tf_op jit(solution)/shard_map/ppermute | solution.py:293
  41.0 2.9 %down.1 = (f32[5,512]{1,0:T(8,128)S(1)}, f32[5,512]{1,0:T(8,128)S(1)}) custom-call(f32[5,2048]{1,0:T(8,128)S(1)} %get-tuple-element.42.x, f32[5,2048]{1,0:T(8,128)S(1)} %bitcast.64, f32[5,5,2048]{2,1,0:T(8,128)S(1)} %get-tuple-element.62.diag, f32[6,5,5,2048]{3,2,1,0:T(8,128)S(1)} %bitcast.50, s32[6,2048]{1,0:T(8,128)S(1)} %bitcast.59, ...), custom_call_target="tpu_custom_call" | custom-call | tf_op jit(solution)/shard_map/down/pallas_call | solution.py:280
  47.7 2.3 %collective-permute-done.13.left = f32[5,512]{1,0:T(8,128)S(1)} collective-permute-done((f32[5,512]{1,0:T(8,128)S(1)}, f32[5,512]{1,0:T(8,128)S(1)}, u32[]{:S(2)}, u32[]{:S(2)}) %collective-permute-start.13) | collective-permute-done | bytes 10272 | tf_op jit(solution)/shard_map/ppermute | solution.py:293
  50.5 5.9 %collective-permute-start.15 = (f32[5,512]{1,0:T(8,128)S(1)}, f32[5,512]{1,0:T(8,128)S(1)}, u32[]{:S(2)}, u32[]{:S(2)}) collective-permute-start(f32[5,512]{1,0:T(8,128)S(1)} %middle_2.1.e), channel_id=1, source_target_pairs={{0,31},{1,0},{2,1},{3,2},{4,3},{5,4},{6,5},{7,6},{8,7},{9,8},{10,9... | collective-permute-start | bytes 30728 | tf_op jit(solution)/shard_map/ppermute | solution.py:293
  59.8 4.3 %collective-permute-start.18 = (f32[5,128]{1,0:T(8,128)S(1)}, f32[5,128]{1,0:T(8,128)S(1)}, u32[]{:S(2)}, u32[]{:S(2)}) collective-permute-start(f32[5,128]{1,0:T(8,128)S(1)} %get-tuple-element.49.field), channel_id=1, source_target_pairs={{0,96},{32,64},{64,32},{96,0},{128,224},{160,192},{192,160},{224,1... | collective-permute-start | bytes 7688 | tf_op jit(solution)/shard_map/ppermute | solution.py:297
  65.0 2.4 %collective-permute-done.19.p2 = f32[5,128]{1,0:T(8,128)S(1)} collective-permute-done((f32[5,128]{1,0:T(8,128)S(1)}, f32[5,128]{1,0:T(8,128)S(1)}, u32[]{:S(2)}, u32[]{:S(2)}) %collective-permute-start.19) | collective-permute-done | bytes 2592 | tf_op jit(solution)/shard_map/ppermute | solution.py:297
  69.2 2.0 %collective-permute-start.23 = (f32[5,128]{1,0:T(8,128)S(1)}, f32[5,128]{1,0:T(8,128)S(1)}, u32[]{:S(2)}, u32[]{:S(2)}) collective-permute-start(f32[5,128]{1,0:T(8,128)S(1)} %coarse_2.1.field), channel_id=1, source_target_pairs={{0,32},{32,0},{64,96},{96,64},{128,160},{160,128},{192,224},{224,1... | collective-permute-start | bytes 7688 | tf_op jit(solution)/shard_map/ppermute | solution.py:297
  72.4 8.0 %collective-permute-start.24 = (f32[5,512]{1,0:T(8,128)S(1)}, f32[5,512]{1,0:T(8,128)S(1)}, u32[]{:S(2)}, u32[]{:S(2)}) collective-permute-start(f32[5,512]{1,0:T(8,128)S(1)} %coarse_3.1.e), channel_id=1, source_target_pairs={{0,31},{1,0},{2,1},{3,2},{4,3},{5,4},{6,5},{7,6},{8,7},{9,8},{10,9... | collective-permute-start | bytes 30728 | tf_op jit(solution)/shard_map/ppermute | solution.py:293
  83.7 3.8 %collective-permute-start.27 = (f32[5,512]{1,0:T(8,128)S(1)}, f32[5,512]{1,0:T(8,128)S(1)}, u32[]{:S(2)}, u32[]{:S(2)}) collective-permute-start(f32[5,512]{1,0:T(8,128)S(1)} %middle_3.1.e), channel_id=1, source_target_pairs={{0,31},{1,0},{2,1},{3,2},{4,3},{5,4},{6,5},{7,6},{8,7},{9,8},{10,9... | collective-permute-start | bytes 30728 | tf_op jit(solution)/shard_map/ppermute | solution.py:293
  91.6 5.9 %collective-permute-start.30 = (f32[5,64]{1,0:T(8,128)S(1)}, f32[5,64]{1,0:T(8,128)S(1)}, u32[]{:S(2)}, u32[]{:S(2)}) collective-permute-start(f32[5,64]{1,0:T(8,128)S(1)} %get-tuple-element.52), channel_id=1, source_target_pairs={{0,30},{1,31},{2,0},{3,1},{4,2},{5,3},{6,4},{7,5},{8,6},{9,7},{10,... | collective-permute-start | bytes 3848 | tf_op jit(solution)/shard_map/ppermute | solution.py:293
  97.5 1.7 %collective-permute-start.32 = (f32[5,64]{1,0:T(8,128)S(1)}, f32[5,64]{1,0:T(8,128)S(1)}, u32[]{:S(2)}, u32[]{:S(2)}) collective-permute-start(f32[5,64]{1,0:T(8,128)S(1)} %get-tuple-element.54), channel_id=1, source_target_pairs={{0,1},{1,2},{2,3},{3,4},{4,5},{5,6},{6,7},{7,8},{8,9},{9,10},{10,1... | collective-permute-start | bytes 3848 | tf_op jit(solution)/shard_map/ppermute | solution.py:293
  100.5 4.5 %collective-permute-done.33.r0 = f32[5,64]{1,0:T(8,128)S(1)} collective-permute-done((f32[5,64]{1,0:T(8,128)S(1)}, f32[5,64]{1,0:T(8,128)S(1)}, u32[]{:S(2)}, u32[]{:S(2)}) %collective-permute-start.33) | collective-permute-done | bytes 1312 | tf_op jit(solution)/shard_map/ppermute | solution.py:293
  105.0 3.4 %fine_4.1 = (f32[5,2048]{1,0:T(8,128)S(1)}, f32[5,64]{1,0:T(8,128)S(1)}, f32[5,64]{1,0:T(8,128)S(1)}, f32[5,64]{1,0:T(8,128)S(1)}, f32[5,64]{1,0:T(8,128)S(1)}) custom-call(f32[5,2048]{1,0:T(8,128)S(1)} %get-tuple-element.51.x, f32[5,2048]{1,0:T(8,128)S(1)} %bitcast.65, f32[5,5,2048]{2,1,0:T(8,128)S(1)} %get-tuple-element.62.diag, ...), custom_call_target="tpu_custom_call" | custom-call | tf_op jit(solution)/shard_map/fine_4/pallas_call | solution.py:280
  108.5 1.7 %collective-permute-start.36 = (f32[5,64]{1,0:T(8,128)S(1)}, f32[5,64]{1,0:T(8,128)S(1)}, u32[]{:S(2)}, u32[]{:S(2)}) collective-permute-start(f32[5,64]{1,0:T(8,128)S(1)} %get-tuple-element.59), channel_id=1, source_target_pairs={{0,1},{1,2},{2,3},{3,4},{4,5},{5,6},{6,7},{7,8},{8,9},{9,10},{10,1... | collective-permute-start | bytes 3848 | tf_op jit(solution)/shard_map/ppermute | solution.py:293
  111.6 4.4 %collective-permute-done.37.r0 = f32[5,64]{1,0:T(8,128)S(1)} collective-permute-done((f32[5,64]{1,0:T(8,128)S(1)}, f32[5,64]{1,0:T(8,128)S(1)}, u32[]{:S(2)}, u32[]{:S(2)}) %collective-permute-start.37) | collective-permute-done | bytes 1312 | tf_op jit(solution)/shard_map/ppermute | solution.py:293
  116.0 3.2 %fine_5.1 = f32[5,2048]{1,0:T(8,128)S(1)} custom-call(f32[5,2048]{1,0:T(8,128)S(1)} %get-tuple-element.56.x, f32[5,2048]{1,0:T(8,128)S(1)} %bitcast.66, f32[5,5,2048]{2,1,0:T(8,128)S(1)} %get-tuple-element.62.diag, f32[5,5,2048]{2,1,0:T(8,128)S(1)} %get-tuple-element.61.inverse, f32[6,5,5,2048]{3,2,1,0:T(8,128)S(1)} %bitcast.52, s32[6,2048]{1,0:T(8,128)S(1)} %bitcast.61, ...), custom_call_target="tpu_custom_call" | custom-call | tf_op jit(solution)/shard_map/fine_5/pallas_call | solution.py:280
  (110 shorter events, 32.7 us)
Async XLA Ops:
  2.9 10.7 %collective-permute-start = (f32[5,64]{1,0:T(8,128)S(1)}, f32[5,64]{1,0:T(8,128)S(1)}, u32[]{:S(2)}, u32[]{:S(2)}) collective-permute-start(f32[5,64]{1,0:T(8,128)S(1)} %get-tuple-element.33), channel_id=1, source_target_pairs={{0,30},{1,31},{2,0},{3,1},{4,2},{5,3},{6,4},{7,5},{8,6},{9,7},{10,... | collective-permute-start | bytes 3848 | tf_op jit(solution)/shard_map/ppermute | solution.py:293
  8.7 4.9 %collective-permute-start.1 = (f32[5,64]{1,0:T(8,128)S(1)}, f32[5,64]{1,0:T(8,128)S(1)}, u32[]{:S(2)}, u32[]{:S(2)}) collective-permute-start(f32[5,64]{1,0:T(8,128)S(1)} %get-tuple-element.34), channel_id=1, source_target_pairs={{0,31},{1,0},{2,1},{3,2},{4,3},{5,4},{6,5},{7,6},{8,7},{9,8},{10,9... | collective-permute-start | bytes 3848 | tf_op jit(solution)/shard_map/ppermute | solution.py:293
  9.7 4.0 %collective-permute-start.2 = (f32[5,64]{1,0:T(8,128)S(1)}, f32[5,64]{1,0:T(8,128)S(1)}, u32[]{:S(2)}, u32[]{:S(2)}) collective-permute-start(f32[5,64]{1,0:T(8,128)S(1)} %get-tuple-element.35), channel_id=1, source_target_pairs={{0,1},{1,2},{2,3},{3,4},{4,5},{5,6},{6,7},{7,8},{8,9},{9,10},{10,1... | collective-permute-start | bytes 3848 | tf_op jit(solution)/shard_map/ppermute | solution.py:293
  10.5 5.8 %collective-permute-start.3 = (f32[5,64]{1,0:T(8,128)S(1)}, f32[5,64]{1,0:T(8,128)S(1)}, u32[]{:S(2)}, u32[]{:S(2)}) collective-permute-start(f32[5,64]{1,0:T(8,128)S(1)} %get-tuple-element.36), channel_id=1, source_target_pairs={{0,2},{1,3},{2,4},{3,5},{4,6},{5,7},{6,8},{7,9},{8,10},{9,11},{10,... | collective-permute-start | bytes 3848 | tf_op jit(solution)/shard_map/ppermute | solution.py:293
  19.6 4.0 %collective-permute-start.4 = (f32[5,64]{1,0:T(8,128)S(1)}, f32[5,64]{1,0:T(8,128)S(1)}, u32[]{:S(2)}, u32[]{:S(2)}) collective-permute-start(f32[5,64]{1,0:T(8,128)S(1)} %get-tuple-element.38), channel_id=1, source_target_pairs={{0,30},{1,31},{2,0},{3,1},{4,2},{5,3},{6,4},{7,5},{8,6},{9,7},{10,... | collective-permute-start | bytes 3848 | tf_op jit(solution)/shard_map/ppermute | solution.py:293
  23.6 5.8 %collective-permute-start.7 = (f32[5,64]{1,0:T(8,128)S(1)}, f32[5,64]{1,0:T(8,128)S(1)}, u32[]{:S(2)}, u32[]{:S(2)}) collective-permute-start(f32[5,64]{1,0:T(8,128)S(1)} %get-tuple-element.41), channel_id=1, source_target_pairs={{0,2},{1,3},{2,4},{3,5},{4,6},{5,7},{6,8},{7,9},{8,10},{9,11},{10,... | collective-permute-start | bytes 3848 | tf_op jit(solution)/shard_map/ppermute | solution.py:293
  32.8 5.9 %collective-permute-start.10 = (f32[5,64]{1,0:T(8,128)S(1)}, f32[5,64]{1,0:T(8,128)S(1)}, u32[]{:S(2)}, u32[]{:S(2)}) collective-permute-start(f32[5,64]{1,0:T(8,128)S(1)} %get-tuple-element.45), channel_id=1, source_target_pairs={{0,1},{1,2},{2,3},{3,4},{4,5},{5,6},{6,7},{7,8},{8,9},{9,10},{10,1... | collective-permute-start | bytes 3848 | tf_op jit(solution)/shard_map/ppermute | solution.py:293
  32.9 6.3 %collective-permute-start.11 = (f32[5,64]{1,0:T(8,128)S(1)}, f32[5,64]{1,0:T(8,128)S(1)}, u32[]{:S(2)}, u32[]{:S(2)}) collective-permute-start(f32[5,64]{1,0:T(8,128)S(1)} %get-tuple-element.46), channel_id=1, source_target_pairs={{0,2},{1,3},{2,4},{3,5},{4,6},{5,7},{6,8},{7,9},{8,10},{9,11},{10,... | collective-permute-start | bytes 3848 | tf_op jit(solution)/shard_map/ppermute | solution.py:293
  33.0 6.3 %collective-permute-start.8 = (f32[5,64]{1,0:T(8,128)S(1)}, f32[5,64]{1,0:T(8,128)S(1)}, u32[]{:S(2)}, u32[]{:S(2)}) collective-permute-start(f32[5,64]{1,0:T(8,128)S(1)} %get-tuple-element.43), channel_id=1, source_target_pairs={{0,30},{1,31},{2,0},{3,1},{4,2},{5,3},{6,4},{7,5},{8,6},{9,7},{10,... | collective-permute-start | bytes 3848 | tf_op jit(solution)/shard_map/ppermute | solution.py:293
  44.0 3.8 %collective-permute-start.12 = (f32[5,512]{1,0:T(8,128)S(1)}, f32[5,512]{1,0:T(8,128)S(1)}, u32[]{:S(2)}, u32[]{:S(2)}) collective-permute-start(f32[5,512]{1,0:T(8,128)S(1)} %get-tuple-element.47.e), channel_id=1, source_target_pairs={{0,31},{1,0},{2,1},{3,2},{4,3},{5,4},{6,5},{7,6},{8,7},{9,8},{10,9... | collective-permute-start | bytes 30728 | tf_op jit(solution)/shard_map/ppermute | solution.py:293
  44.4 5.7 %collective-permute-start.13 = (f32[5,512]{1,0:T(8,128)S(1)}, f32[5,512]{1,0:T(8,128)S(1)}, u32[]{:S(2)}, u32[]{:S(2)}) collective-permute-start(f32[5,512]{1,0:T(8,128)S(1)} %get-tuple-element.47.e), channel_id=1, source_target_pairs={{0,1},{1,2},{2,3},{3,4},{4,5},{5,6},{6,7},{7,8},{8,9},{9,10},{10,1... | collective-permute-start | bytes 30728 | tf_op jit(solution)/shard_map/ppermute | solution.py:293
  46.0 4.1 %collective-permute-start.14 = (f32[5,512]{1,0:T(8,128)S(1)}, f32[5,512]{1,0:T(8,128)S(1)}, u32[]{:S(2)}, u32[]{:S(2)}) collective-permute-start(f32[5,512]{1,0:T(8,128)S(1)} %get-tuple-element.47.e), channel_id=1, source_target_pairs={{0,32},{32,0},{64,96},{96,64},{128,160},{160,128},{192,224},{224,1... | collective-permute-start | bytes 30728 | tf_op jit(solution)/shard_map/ppermute | solution.py:297
  50.5 7.5 %collective-permute-start.15 = (f32[5,512]{1,0:T(8,128)S(1)}, f32[5,512]{1,0:T(8,128)S(1)}, u32[]{:S(2)}, u32[]{:S(2)}) collective-permute-start(f32[5,512]{1,0:T(8,128)S(1)} %middle_2.1.e), channel_id=1, source_target_pairs={{0,31},{1,0},{2,1},{3,2},{4,3},{5,4},{6,5},{7,6},{8,7},{9,8},{10,9... | collective-permute-start | bytes 30728 | tf_op jit(solution)/shard_map/ppermute | solution.py:293
  59.8 5.3 %collective-permute-start.18 = (f32[5,128]{1,0:T(8,128)S(1)}, f32[5,128]{1,0:T(8,128)S(1)}, u32[]{:S(2)}, u32[]{:S(2)}) collective-permute-start(f32[5,128]{1,0:T(8,128)S(1)} %get-tuple-element.49.field), channel_id=1, source_target_pairs={{0,96},{32,64},{64,32},{96,0},{128,224},{160,192},{192,160},{224,1... | collective-permute-start | bytes 7688 | tf_op jit(solution)/shard_map/ppermute | solution.py:297
  64.0 3.4 %collective-permute-start.19 = (f32[5,128]{1,0:T(8,128)S(1)}, f32[5,128]{1,0:T(8,128)S(1)}, u32[]{:S(2)}, u32[]{:S(2)}) collective-permute-start(f32[5,128]{1,0:T(8,128)S(1)} %get-tuple-element.49.field), channel_id=1, source_target_pairs={{0,64},{32,96},{64,0},{96,32},{128,192},{160,224},{192,128},{224,1... | collective-permute-start | bytes 7688 | tf_op jit(solution)/shard_map/ppermute | solution.py:297
  64.0 3.4 %collective-permute-start.20 = (f32[5,128]{1,0:T(8,128)S(1)}, f32[5,128]{1,0:T(8,128)S(1)}, u32[]{:S(2)}, u32[]{:S(2)}) collective-permute-start(f32[5,128]{1,0:T(8,128)S(1)} %get-tuple-element.49.field), channel_id=1, source_target_pairs={{0,32},{32,0},{64,96},{96,64},{128,160},{160,128},{192,224},{224,1... | collective-permute-start | bytes 7688 | tf_op jit(solution)/shard_map/ppermute | solution.py:297
  67.5 4.3 %collective-permute-start.21 = (f32[5,128]{1,0:T(8,128)S(1)}, f32[5,128]{1,0:T(8,128)S(1)}, u32[]{:S(2)}, u32[]{:S(2)}) collective-permute-start(f32[5,128]{1,0:T(8,128)S(1)} %coarse_2.1.field), channel_id=1, source_target_pairs={{0,96},{32,64},{64,32},{96,0},{128,224},{160,192},{192,160},{224,1... | collective-permute-start | bytes 7688 | tf_op jit(solution)/shard_map/ppermute | solution.py:297
  68.8 3.4 %collective-permute-start.22 = (f32[5,128]{1,0:T(8,128)S(1)}, f32[5,128]{1,0:T(8,128)S(1)}, u32[]{:S(2)}, u32[]{:S(2)}) collective-permute-start(f32[5,128]{1,0:T(8,128)S(1)} %coarse_2.1.field), channel_id=1, source_target_pairs={{0,64},{32,96},{64,0},{96,32},{128,192},{160,224},{192,128},{224,1... | collective-permute-start | bytes 7688 | tf_op jit(solution)/shard_map/ppermute | solution.py:297
  72.4 9.7 %collective-permute-start.24 = (f32[5,512]{1,0:T(8,128)S(1)}, f32[5,512]{1,0:T(8,128)S(1)}, u32[]{:S(2)}, u32[]{:S(2)}) collective-permute-start(f32[5,512]{1,0:T(8,128)S(1)} %coarse_3.1.e), channel_id=1, source_target_pairs={{0,31},{1,0},{2,1},{3,2},{4,3},{5,4},{6,5},{7,6},{8,7},{9,8},{10,9... | collective-permute-start | bytes 30728 | tf_op jit(solution)/shard_map/ppermute | solution.py:293
  83.7 5.5 %collective-permute-start.27 = (f32[5,512]{1,0:T(8,128)S(1)}, f32[5,512]{1,0:T(8,128)S(1)}, u32[]{:S(2)}, u32[]{:S(2)}) collective-permute-start(f32[5,512]{1,0:T(8,128)S(1)} %middle_3.1.e), channel_id=1, source_target_pairs={{0,31},{1,0},{2,1},{3,2},{4,3},{5,4},{6,5},{7,6},{8,7},{9,8},{10,9... | collective-permute-start | bytes 30728 | tf_op jit(solution)/shard_map/ppermute | solution.py:293
  91.6 7.6 %collective-permute-start.30 = (f32[5,64]{1,0:T(8,128)S(1)}, f32[5,64]{1,0:T(8,128)S(1)}, u32[]{:S(2)}, u32[]{:S(2)}) collective-permute-start(f32[5,64]{1,0:T(8,128)S(1)} %get-tuple-element.52), channel_id=1, source_target_pairs={{0,30},{1,31},{2,0},{3,1},{4,2},{5,3},{6,4},{7,5},{8,6},{9,7},{10,... | collective-permute-start | bytes 3848 | tf_op jit(solution)/shard_map/ppermute | solution.py:293
  99.2 5.8 %collective-permute-start.33 = (f32[5,64]{1,0:T(8,128)S(1)}, f32[5,64]{1,0:T(8,128)S(1)}, u32[]{:S(2)}, u32[]{:S(2)}) collective-permute-start(f32[5,64]{1,0:T(8,128)S(1)} %get-tuple-element.55), channel_id=1, source_target_pairs={{0,2},{1,3},{2,4},{3,5},{4,6},{5,7},{6,8},{7,9},{8,10},{9,11},{10,... | collective-permute-start | bytes 3848 | tf_op jit(solution)/shard_map/ppermute | solution.py:293
  108.4 3.2 %collective-permute-start.34 = (f32[5,64]{1,0:T(8,128)S(1)}, f32[5,64]{1,0:T(8,128)S(1)}, u32[]{:S(2)}, u32[]{:S(2)}) collective-permute-start(f32[5,64]{1,0:T(8,128)S(1)} %get-tuple-element.57), channel_id=1, source_target_pairs={{0,30},{1,31},{2,0},{3,1},{4,2},{5,3},{6,4},{7,5},{8,6},{9,7},{10,... | collective-permute-start | bytes 3848 | tf_op jit(solution)/shard_map/ppermute | solution.py:293
  110.3 5.8 %collective-permute-start.37 = (f32[5,64]{1,0:T(8,128)S(1)}, f32[5,64]{1,0:T(8,128)S(1)}, u32[]{:S(2)}, u32[]{:S(2)}) collective-permute-start(f32[5,64]{1,0:T(8,128)S(1)} %get-tuple-element.60), channel_id=1, source_target_pairs={{0,2},{1,3},{2,4},{3,5},{4,6},{5,7},{6,8},{7,9},{8,10},{9,11},{10,... | collective-permute-start | bytes 3848 | tf_op jit(solution)/shard_map/ppermute | solution.py:293
  (30 other events, 239.6 us)
where the time goes:
time: 120 us
  starting transfers between devices  62.9 us (52%)
  waiting for transfers between devices  30.4 us (25%)
  Pallas kernels  20.1 us (17%)
  local copies, waits for them, and re-layouts  6.05 us (5%)
    ppermute x28, starting transfers between devices, passed_along(): return lax.ppermute(x, 'dom', [(i, (i + by) % size) for i in range(size)])  48 us
    ppermute x28, waiting for transfers between devices, passed_along(): return lax.ppermute(x, 'dom', [(i, (i + by) % size) for i in range(size)])  23.8 us
    pallas_call x12, Pallas kernels, call(): pl.pallas_call(kernel, name=name, out_shape=[jax.ShapeDtypeStruct(s, F32)...  20.1 us
    ppermute x10, starting transfers between devices, group_swap(): lax.ppermute(x, 'grp', [(i, i ^ mask) for i in range(lax.axis_size('grp'))])  15 us
    ppermute x10, waiting for transfers between devices, group_swap(): lax.ppermute(x, 'grp', [(i, i ^ mask) for i in range(lax.axis_size('grp'))])  6.57 us
    unnamed x42, local copies, waits for them, and re-layouts  3.47 us
  transfers between devices with their start and end apart: 38, of which 18 were waited for; matrix products, arithmetic and copies ran while one was open for 3% of the time, Pallas kernels for 0%

commit v1 on v0

v1 whole, which is shorter than its diff:
```python
import functools

import jax
import jax.numpy as jnp
from jax import lax
from jax.experimental import pallas as pl
from jax.experimental.pallas import tpu as pltpu
from jax.sharding import PartitionSpec as P

ROWS_FINE = 2048
ROWS_MID = 512
ROWS_COARSE = 128
SLOT_ROWS = 64
RIM_ROWS = 32
LANES = 128
OFFSETS = (-2, -1, 1, 2)
RELAX = 0.8
F32 = jnp.float32


def lane_pick(chunk, index):
    return jnp.take_along_axis(chunk, index, axis=1, mode="promise_in_bounds")


def decode(index, chunks):
    low = index & (LANES - 1)
    odd = [(index & (LANES << bit)) != 0 for bit in range((chunks - 1).bit_length())]
    return low, odd


def pick(table, decoded, chunks):
    low, odd = decoded
    level = [lane_pick(jnp.broadcast_to(table(t), low.shape), low) for t in range(chunks)]
    for bit in odd:
        level = [
            jnp.where(bit, level[i + 1], level[i]) if i + 1 < len(level) else level[i]
            for i in range(0, len(level), 2)
        ]
    return level[0]


def product(total, blocks, vectors):
    result = []
    for i in range(5):
        value = total[i] if total is not None else None
        for k in range(5):
            term = blocks(i, k) * vectors[k]
            value = term if value is None else value + term
        result.append(value)
    return result


def apply_dense(diag, coupling, columns, own, table, chunks, rows, remap=None):
    image = product(None, lambda i, k: diag[i, k, rows, :], own)
    for n in range(6):
        index = columns[n, rows, :]
        if remap is not None:
            index = remap(index)
        decoded = decode(index, chunks)
        picked = [pick(functools.partial(table, k), decoded, chunks) for k in range(5)]
        image = product(image, lambda i, k: coupling[n, i, k, rows, :], picked)
    return image


def padded(value):
    return jnp.concatenate([value, jnp.zeros((3, value.shape[1]), value.dtype)], axis=0)


def rows_of(parts):
    return jnp.concatenate([jnp.sum(part, axis=0, keepdims=True) for part in parts], axis=0)


def channels(field, group):
    zero = jnp.zeros((3, LANES), F32)
    return jnp.concatenate([field[k, group : group + 1, :] for k in range(5)] + [zero], axis=0)


def split3(value):
    first = value.astype(jnp.bfloat16)
    rest = value - first.astype(F32)
    second = rest.astype(jnp.bfloat16)
    third = (rest - second.astype(F32)).astype(jnp.bfloat16)
    return first, second, third


def restrict(residual, aggregate, number, store):
    groups = number // LANES
    total = jnp.zeros((3 * 8 * groups, LANES), F32)
    step = 4 * LANES
    for start in range(0, residual.shape[1], 4):
        parts = range(start, start + 4)
        index = jnp.concatenate([aggregate[g : g + 1, :] for g in parts], axis=1)
        value = jnp.concatenate([channels(residual, g) for g in parts], axis=1)
        high = index >> 7
        low = index & (LANES - 1)
        left = []
        for piece in split3(value):
            wide = piece.astype(F32)
            left += [jnp.where(high == h, wide, 0.0) for h in range(groups)]
        left = jnp.concatenate(left, axis=0).astype(jnp.bfloat16)
        lanes = lax.broadcasted_iota(jnp.int32, (LANES, step), 0)
        hot = jnp.where(lanes == low, 1.0, 0.0).astype(jnp.bfloat16)
        total = total + lax.dot_general(
            left, hot, (((1,), (1,)), ((), ())), preferred_element_type=F32
        )
    size = 8 * groups
    summed = total[:size] + total[size : 2 * size] + total[2 * size :]
    for h in range(groups):
        store(h, summed[h * 8 : h * 8 + 8])


HALVES = (slice(0, 8), slice(8, 16))


def fine_table(x, received):
    r3, r2, r1, r0 = received
    low, high = r0[...] + r1[...], r2[...] + r3[...]

    def table(k, t):
        if t < 16:
            return x[k, t : t + 1, :]
        return (low, high)[t - 16][k : k + 1]

    return table


def pack_sends(x, where, live, outs):
    decoded = decode(where[...], 16)
    for k in range(5):
        picked = pick(lambda t: x[k, t : t + 1, :], decoded, 16) * live[...]
        for j in range(4):
            outs[j][k : k + 1, :] = picked[j : j + 1, :]


def send_kernel(x, send, count, s0, s1, s2, s3, where, live):
    lane = lax.broadcasted_iota(jnp.int32, (1, LANES), 1)
    for j in range(4):
        first = SLOT_ROWS * ((3 - j) % 2)
        row = send[j : j + 1, :]
        where[j : j + 1, :] = jnp.concatenate([row, row], axis=1)
        inside = (lane >= first) & (lane < first + count[j])
        live[j : j + 1, :] = jnp.where(inside, 1.0, 0.0)
    pack_sends(x, where, live, (s0, s1, s2, s3))


def fine_kernel(last, x, b, diag, inverse, coupling, columns, where, live, r3, r2, r1, r0, *rest):
    if last:
        (new,) = rest
    else:
        s0, s1, s2, s3, new = rest
    table = fine_table(x, (r3, r2, r1, r0))
    for rows in HALVES:
        own = [x[k, rows, :] for k in range(5)]
        image = apply_dense(diag, coupling, columns, own, table, 18, rows)
        left = [b[k, rows, :] - image[k] for k in range(5)]
        change = product(None, lambda i, k: inverse[i, k, rows, :], left)
        for k in range(5):
            new[k, rows, :] = own[k] + RELAX * change[k]
    if not last:
        pack_sends(new, where, live, (s0, s1, s2, s3))


def down_kernel(
    x, b, diag, coupling, columns, aggregate, m_inverse, r3, r2, r1, r0, rhs, e, residual
):
    table = fine_table(x, (r3, r2, r1, r0))
    for rows in HALVES:
        own = [x[k, rows, :] for k in range(5)]
        image = apply_dense(diag, coupling, columns, own, table, 18, rows)
        for k in range(5):
            residual[k, rows, :] = b[k, rows, :] - image[k]

    def store(h, value):
        for k in range(5):
            rhs[k, h : h + 1, :] = value[k : k + 1]

    restrict(residual, aggregate, ROWS_MID, store)
    change = product(None, lambda i, k: m_inverse[i, k], [rhs[k] for k in range(5)])
    for k in range(5):
        e[k] = RELAX * change[k]


def middle_remap(index):
    left = index + (8 * LANES + LANES - RIM_ROWS)
    own = index - RIM_ROWS
    right = index + (9 * LANES - RIM_ROWS - ROWS_MID)
    partner = index - 2 * RIM_ROWS
    return jnp.where(
        index < RIM_ROWS,
        left,
        jnp.where(
            index < RIM_ROWS + ROWS_MID,
            own,
            jnp.where(index < 2 * RIM_ROWS + ROWS_MID, right, partner),
        ),
    )


def middle_image(e, right, left, partner, diag, coupling, columns):
    def table(k, t):
        if t < 4:
            return e[k, t : t + 1, :]
        if t < 8:
            return partner[k, t - 4 : t - 3, :]
        return left[k, 3:4, :] if t == 8 else right[k, 0:1, :]

    own = [e[k] for k in range(5)]
    return own, apply_dense(diag, coupling, columns, own, table, 10, slice(0, 4), middle_remap)


def middle_update(e, rhs, diag, inverse, coupling, columns, right, left, partner):
    own, image = middle_image(e, right, left, partner, diag, coupling, columns)
    gap = [rhs[k] - image[k] for k in range(5)]
    change = product(None, lambda i, k: inverse[i, k], gap)
    return [own[k] + RELAX * change[k] for k in range(5)]


def middle_kernel(e, rhs, diag, inverse, coupling, columns, right, left, partner, new):
    done = middle_update(e, rhs, diag, inverse, coupling, columns, right, left, partner)
    for k in range(5):
        new[k] = done[k]


def coarse_down_kernel(
    e, rhs, diag, coupling, columns, right, left, partner, aggregate, c_inverse, c_rhs, c_new, residual
):
    own, image = middle_image(e, right, left, partner, diag, coupling, columns)
    for k in range(5):
        residual[k] = rhs[k] - image[k]

    def store(h, value):
        c_rhs[...] = value[:5]
        c_new[...] = RELAX * rows_of([c_inverse[i] * value[:5] for i in range(5)])

    restrict(residual, aggregate, ROWS_COARSE, store)


def coarse_rows(field, others, diag, inverse, coupling, columns, rhs):
    own = field[...]
    members = [padded(r[...]) for r in (field,) + others]
    parts = [diag[i] * own for i in range(5)]
    for n in range(6):
        decoded = decode(jnp.broadcast_to(columns[n : n + 1, :], (8, LANES)), 4)
        picked = pick(lambda t: members[t], decoded, 4)[:5]
        for i in range(5):
            parts[i] = parts[i] + coupling[n, i] * picked
    gap = rhs[...] - rows_of(parts)
    return own + RELAX * rows_of([inverse[i] * gap for i in range(5)])


def coarse_kernel(field, rhs, diag, inverse, coupling, columns, p3, p2, p1, new):
    new[...] = coarse_rows(field, (p1, p2, p3), diag, inverse, coupling, columns, rhs)


def coarse_up_kernel(field, rhs, diag, inverse, coupling, columns, p3, p2, p1, e, aggregate, new):
    done = coarse_rows(field, (p1, p2, p3), diag, inverse, coupling, columns, rhs)
    decoded = decode(aggregate[...], 1)
    for k in range(5):
        new[k] = e[k] + pick(lambda t: done[k : k + 1], decoded, 1)


def middle_up_kernel(
    e, rhs, diag, inverse, coupling, columns, right, left, partner, x, aggregate, where, live,
    s0, s1, s2, s3, new
):
    done = middle_update(e, rhs, diag, inverse, coupling, columns, right, left, partner)
    for rows in HALVES:
        decoded = decode(aggregate[rows, :], 4)
        for k in range(5):
            new[k, rows, :] = x[k, rows, :] + pick(lambda t: done[k][t : t + 1], decoded, 4)
    pack_sends(new, where, live, (s0, s1, s2, s3))


VMEM = pl.BlockSpec(memory_space=pltpu.VMEM)
SMEM = pl.BlockSpec(memory_space=pltpu.SMEM)


def call(name, kernel, args, shapes, scratch=(), scalars=()):
    return pl.pallas_call(
        kernel,
        name=name,
        out_shape=[s if isinstance(s, jax.ShapeDtypeStruct) else jax.ShapeDtypeStruct(s, F32) for s in shapes],
        in_specs=[SMEM if i in scalars else VMEM for i in range(len(args))],
        out_specs=[VMEM] * len(shapes),
        scratch_shapes=[pltpu.VMEM(s, F32) for s in scratch],
        compiler_params=pltpu.CompilerParams(vmem_limit_bytes=16 * 1024 * 1024),
    )(*args)


def passed_along(x, by):
    size = lax.axis_size("dom")
    return lax.ppermute(x, "dom", [(i, (i + by) % size) for i in range(size)])


def group_swap(x, mask):
    return lax.ppermute(x, "grp", [(i, i ^ mask) for i in range(lax.axis_size("grp"))])


def per_device(
    right_side, initial_guess, fine_diag, fine_inverse, fine_coupling, fine_columns, fine_send, fine_count,
    fine_aggregate, middle_diag, middle_inverse, middle_coupling, middle_columns, middle_aggregate,
    coarse_diag, coarse_inverse, coarse_coupling, coarse_columns,
):
    def dense(array):
        return array.reshape(array.shape[2:-1] + (array.shape[-1] // LANES, LANES))

    b, x = dense(right_side), dense(initial_guess)
    f_mats = tuple(map(dense, (fine_diag, fine_inverse, fine_coupling, fine_columns)))
    f_send, f_count, f_aggregate = fine_send[0, 0], fine_count[0, 0], dense(fine_aggregate)
    m_mats = tuple(map(dense, (middle_diag, middle_inverse, middle_coupling, middle_columns)))
    m_aggregate = dense(middle_aggregate)
    c_mats = (coarse_diag[0, 0], coarse_inverse[0, 0], coarse_coupling[0, 0], coarse_columns[0, 0])

    slots = [(5, LANES)] * 4
    fine = (5, ROWS_FINE // LANES, LANES)
    mid = (5, ROWS_MID // LANES, LANES)
    coarse = (5, ROWS_COARSE)

    def fine_exchange(sends):
        return [passed_along(sends[3 - j], -OFFSETS[j]) for j in (3, 2, 1, 0)]

    def middle_exchange(e):
        right = passed_along(e, -1)
        left = passed_along(e, 1)
        return [right, left, group_swap(e, 1)]

    def coarse_exchange(c):
        return [group_swap(c, mask) for mask in (3, 2, 1)]

    *sends, where, live = call(
        "send", send_kernel, (x, f_send, f_count),
        slots + [jax.ShapeDtypeStruct((4, LANES), jnp.int32), (4, LANES)], scalars=(2,),
    )

    def fine_sweep(name, x, sends, last=False):
        out = call(
            name,
            functools.partial(fine_kernel, last),
            (x, b) + f_mats + (where, live, *fine_exchange(sends)),
            [fine] if last else slots + [fine],
        )
        return out[-1], out[:-1]

    x, sends = fine_sweep("fine_1", x, sends)
    x, sends = fine_sweep("fine_2", x, sends)
    rhs, e = call(
        "down",
        down_kernel,
        (x, b, f_mats[0], f_mats[2], f_mats[3], f_aggregate, m_mats[1], *fine_exchange(sends)),
        [mid, mid],
        [fine],
    )

    def middle_sweep(name, e):
        return call(name, middle_kernel, (e, rhs) + m_mats + tuple(middle_exchange(e)), [mid])[0]

    e = middle_sweep("middle_2", e)
    c_rhs, c = call(
        "coarse_down",
        coarse_down_kernel,
        (e, rhs, m_mats[0], m_mats[2], m_mats[3], *middle_exchange(e), m_aggregate, c_mats[1]),
        [coarse, coarse],
        [mid],
    )
    (c,) = call("coarse_2", coarse_kernel, (c, c_rhs) + c_mats + tuple(coarse_exchange(c)), [coarse])
    (e,) = call(
        "coarse_3",
        coarse_up_kernel,
        (c, c_rhs) + c_mats + tuple(coarse_exchange(c)) + (e, m_aggregate),
        [mid],
    )
    e = middle_sweep("middle_3", e)
    *sends, x = call(
        "middle_4",
        middle_up_kernel,
        (e, rhs) + m_mats + tuple(middle_exchange(e)) + (x, f_aggregate, where, live),
        slots + [fine],
    )
    x, sends = fine_sweep("fine_4", x, sends)
    x, _ = fine_sweep("fine_5", x, sends, last=True)
    return x.reshape(1, 1, 5, ROWS_FINE)


def solution(mesh):
    def spec(rank):
        return P("grp", "dom", *([None] * (rank - 2)))

    ranks = (4, 4, 5, 5, 6, 4, 4, 3, 3, 5, 5, 6, 4, 3, 5, 5, 6, 4)
    return jax.shard_map(
        per_device,
        mesh=mesh,
        in_specs=tuple(spec(rank) for rank in ranks),
        out_specs=spec(4),
        check_vma=False,
    )
```

time: 120 us -> 115 us (0.958)
  Pallas kernels: 20.1 us -> 11.3 us
  waiting for transfers between devices: 30.4 us -> 35.7 us
  starting transfers between devices: 62.9 us -> 60.7 us
    pallas_call x12, Pallas kernels: 20.1 us -> 11.3 us  [call(): pl.pallas_call(kernel, name=name, out_shape=[s if isinstance(s, jax.Shape...]
    ppermute x28, waiting for transfers between devices: 23.8 us -> 29.9 us  [passed_along(): return lax.ppermute(x, 'dom', [(i, (i + by) % size) for i in range(size)])]
    unnamed x42 -> x49, local copies, waits for them, and re-layouts: 3.47 us -> 6.93 us
    ppermute x10, starting transfers between devices: 15 us -> 12.1 us  [group_swap(): lax.ppermute(x, 'grp', [(i, i ^ mask) for i in range(lax.axis_size('grp'))])]
    squeeze x2 -> x0, local copies, waits for them, and re-layouts: 1.92 us -> none  [the longest x1 1.85 us: per_device(): fine_coupling[0, 0]]
  transfers between devices with their start and end apart: 38 -> 38, of which waited for: 18 -> 21; matrix products, arithmetic and copies ran while one was open for 3% -> 0% of each run, Pallas kernels for 0% -> 0%
where the time goes in v1:
time: 115 us
  starting transfers between devices  60.7 us (53%)
  waiting for transfers between devices  35.7 us (31%)
  Pallas kernels  11.3 us (10%)
  local copies, waits for them, and re-layouts  6.94 us (6%)
    ppermute x28, starting transfers between devices, passed_along(): return lax.ppermute(x, 'dom', [(i, (i + by) % size) for i in range(size)])  48.6 us
    ppermute x28, waiting for transfers between devices, passed_along(): return lax.ppermute(x, 'dom', [(i, (i + by) % size) for i in range(size)])  29.9 us
    ppermute x10, starting transfers between devices, group_swap(): lax.ppermute(x, 'grp', [(i, i ^ mask) for i in range(lax.axis_size('grp'))])  12.1 us
    pallas_call x12, Pallas kernels, call(): pl.pallas_call(kernel, name=name, out_shape=[s if isinstance(s, jax.Shape...  11.3 us
    unnamed x49, local copies, waits for them, and re-layouts  6.93 us
    ppermute x10, waiting for transfers between devices, group_swap(): lax.ppermute(x, 'grp', [(i, i ^ mask) for i in range(lax.axis_size('grp'))])  5.79 us
  transfers between devices with their start and end apart: 38, of which 21 were waited for; matrix products, arithmetic and copies ran while one was open for 0% of the time, Pallas kernels for 0%

profile of v1, /device:TPU:1, one launch (start us, length us, event | category | flops | bytes accessed | tf_op | source)
XLA Modules:
  0.0 115.0 jit_solution(6345391893616575191)
XLA Ops:
  2.9 5.8 %collective-permute-start = (f32[5,128]{1,0:T(8,128)S(1)}, f32[5,128]{1,0:T(8,128)S(1)}, u32[]{:S(2)}, u32[]{:S(2)}) collective-permute-start(f32[5,128]{1,0:T(8,128)S(1)} %get-tuple-element.37), channel_id=1, source_target_pairs={{0,30},{1,31},{2,0},{3,1},{4,2},{5,3},{6,4},{7,5},{8,6},{9,7},{10,... | collective-permute-start | bytes 7688 | tf_op jit(solution)/shard_map/ppermute | solution.py:292
  11.8 4.5 %collective-permute-done.3.r0 = f32[5,128]{1,0:T(8,128)S(1)} collective-permute-done((f32[5,128]{1,0:T(8,128)S(1)}, f32[5,128]{1,0:T(8,128)S(1)}, u32[]{:S(2)}, u32[]{:S(2)}) %collective-permute-start.3) | collective-permute-done | bytes 2592 | tf_op jit(solution)/shard_map/ppermute | solution.py:292
  23.6 1.5 %collective-permute-start.6 = (f32[5,128]{1,0:T(8,128)S(1)}, f32[5,128]{1,0:T(8,128)S(1)}, u32[]{:S(2)}, u32[]{:S(2)}) collective-permute-start(f32[5,128]{1,0:T(8,128)S(1)} %get-tuple-element.44), channel_id=1, source_target_pairs={{0,1},{1,2},{2,3},{3,4},{4,5},{5,6},{6,7},{7,8},{8,9},{9,10},{10,1... | collective-permute-start | bytes 7688 | tf_op jit(solution)/shard_map/ppermute | solution.py:292
  26.7 4.2 %collective-permute-done.7.r0 = f32[5,128]{1,0:T(8,128)S(1)} collective-permute-done((f32[5,128]{1,0:T(8,128)S(1)}, f32[5,128]{1,0:T(8,128)S(1)}, u32[]{:S(2)}, u32[]{:S(2)}) %collective-permute-start.7) | collective-permute-done | bytes 2592 | tf_op jit(solution)/shard_map/ppermute | solution.py:292
  32.7 1.6 %collective-permute-start.10 = (f32[5,128]{1,0:T(8,128)S(1)}, f32[5,128]{1,0:T(8,128)S(1)}, u32[]{:S(2)}, u32[]{:S(2)}) collective-permute-start(f32[5,128]{1,0:T(8,128)S(1)} %get-tuple-element.49), channel_id=1, source_target_pairs={{0,1},{1,2},{2,3},{3,4},{4,5},{5,6},{6,7},{7,8},{8,9},{9,10},{10,1... | collective-permute-start | bytes 7688 | tf_op jit(solution)/shard_map/ppermute | solution.py:292
  35.9 4.3 %collective-permute-done.11.r0 = f32[5,128]{1,0:T(8,128)S(1)} collective-permute-done((f32[5,128]{1,0:T(8,128)S(1)}, f32[5,128]{1,0:T(8,128)S(1)}, u32[]{:S(2)}, u32[]{:S(2)}) %collective-permute-start.11) | collective-permute-done | bytes 2592 | tf_op jit(solution)/shard_map/ppermute | solution.py:292
  40.2 1.6 %down.1 = (f32[5,4,128]{2,1,0:T(4,128)S(1)}, f32[5,4,128]{2,1,0:T(4,128)S(1)}) custom-call(f32[5,16,128]{2,1,0:T(8,128)S(1)} %get-tuple-element.46.x, f32[5,16,128]{2,1,0:T(8,128)S(1)} %bitcast.55, f32[5,5,16,128]{3,2,1,0:T(8,128)S(1)} %bitcast.35, f32[6,5,5,16,128]{4,3,2,1,0:T(8,128)S(1)} %bitcast.30, s32[6,16,128]{2,1,0:T(8,128)S(1)} %bitcast.48, ...), custom_call_target="tpu_custom_call" | custom-call | tf_op jit(solution)/shard_map/down/pallas_call | solution.py:279
  41.8 1.7 %collective-permute-start.14 = (f32[5,4,128]{2,1,0:T(4,128)S(1)}, f32[5,4,128]{2,1,0:T(4,128)S(1)}, u32[]{:S(2)}, u32[]{:S(2)}) collective-permute-start(f32[5,4,128]{2,1,0:T(4,128)S(1)} %get-tuple-element.51.e), channel_id=1, source_target_pairs={{0,32},{32,0},{64,96},{96,64},{128,160},{160,128},{192,224},{224,1... | collective-permute-start | bytes 30728 | tf_op jit(solution)/shard_map/ppermute | solution.py:296
  44.7 1.9 %collective-permute-done.12.right = f32[5,4,128]{2,1,0:T(4,128)S(1)} collective-permute-done((f32[5,4,128]{2,1,0:T(4,128)S(1)}, f32[5,4,128]{2,1,0:T(4,128)S(1)}, u32[]{:S(2)}, u32[]{:S(2)}) %collective-permute-start.12) | collective-permute-done | bytes 10272 | tf_op jit(solution)/shard_map/ppermute | solution.py:292
  47.7 3.4 %collective-permute-start.15 = (f32[5,4,128]{2,1,0:T(4,128)S(1)}, f32[5,4,128]{2,1,0:T(4,128)S(1)}, u32[]{:S(2)}, u32[]{:S(2)}) collective-permute-start(f32[5,4,128]{2,1,0:T(4,128)S(1)} %middle_2.1.e), channel_id=1, source_target_pairs={{0,31},{1,0},{2,1},{3,2},{4,3},{5,4},{6,5},{7,6},{8,7},{9,8},{10,9... | collective-permute-start | bytes 30728 | tf_op jit(solution)/shard_map/ppermute | solution.py:292
  52.5 1.7 %collective-permute-start.20 = (f32[5,128]{1,0:T(8,128)S(1)}, f32[5,128]{1,0:T(8,128)S(1)}, u32[]{:S(2)}, u32[]{:S(2)}) collective-permute-start(f32[5,128]{1,0:T(8,128)S(1)} %get-tuple-element.53.field), channel_id=1, source_target_pairs={{0,32},{32,0},{64,96},{96,64},{128,160},{160,128},{192,224},{224,1... | collective-permute-start | bytes 7688 | tf_op jit(solution)/shard_map/ppermute | solution.py:296
  54.1 3.0 %collective-permute-start.19 = (f32[5,128]{1,0:T(8,128)S(1)}, f32[5,128]{1,0:T(8,128)S(1)}, u32[]{:S(2)}, u32[]{:S(2)}) collective-permute-start(f32[5,128]{1,0:T(8,128)S(1)} %get-tuple-element.53.field), channel_id=1, source_target_pairs={{0,64},{32,96},{64,0},{96,32},{128,192},{160,224},{192,128},{224,1... | collective-permute-start | bytes 7688 | tf_op jit(solution)/shard_map/ppermute | solution.py:296
  58.1 3.3 %collective-permute-done.18.p3 = f32[5,128]{1,0:T(8,128)S(1)} collective-permute-done((f32[5,128]{1,0:T(8,128)S(1)}, f32[5,128]{1,0:T(8,128)S(1)}, u32[]{:S(2)}, u32[]{:S(2)}) %collective-permute-start.18) | collective-permute-done | bytes 2592 | tf_op jit(solution)/shard_map/ppermute | solution.py:296
  61.9 3.2 %collective-permute-start.21 = (f32[5,128]{1,0:T(8,128)S(1)}, f32[5,128]{1,0:T(8,128)S(1)}, u32[]{:S(2)}, u32[]{:S(2)}) collective-permute-start(f32[5,128]{1,0:T(8,128)S(1)} %coarse_2.1.field), channel_id=1, source_target_pairs={{0,96},{32,64},{64,32},{96,0},{128,224},{160,192},{192,160},{224,1... | collective-permute-start | bytes 7688 | tf_op jit(solution)/shard_map/ppermute | solution.py:296
  66.7 2.1 %collective-permute-start.25 = (f32[5,4,128]{2,1,0:T(4,128)S(1)}, f32[5,4,128]{2,1,0:T(4,128)S(1)}, u32[]{:S(2)}, u32[]{:S(2)}) collective-permute-start(f32[5,4,128]{2,1,0:T(4,128)S(1)} %coarse_3.1.e), channel_id=1, source_target_pairs={{0,1},{1,2},{2,3},{3,4},{4,5},{5,6},{6,7},{7,8},{8,9},{9,10},{10,1... | collective-permute-start | bytes 30728 | tf_op jit(solution)/shard_map/ppermute | solution.py:292
  68.7 6.9 %collective-permute-start.24 = (f32[5,4,128]{2,1,0:T(4,128)S(1)}, f32[5,4,128]{2,1,0:T(4,128)S(1)}, u32[]{:S(2)}, u32[]{:S(2)}) collective-permute-start(f32[5,4,128]{2,1,0:T(4,128)S(1)} %coarse_3.1.e), channel_id=1, source_target_pairs={{0,31},{1,0},{2,1},{3,2},{4,3},{5,4},{6,5},{7,6},{8,7},{9,8},{10,9... | collective-permute-start | bytes 30728 | tf_op jit(solution)/shard_map/ppermute | solution.py:292
  77.0 1.5 %collective-permute-start.29 = (f32[5,4,128]{2,1,0:T(4,128)S(1)}, f32[5,4,128]{2,1,0:T(4,128)S(1)}, u32[]{:S(2)}, u32[]{:S(2)}) collective-permute-start(f32[5,4,128]{2,1,0:T(4,128)S(1)} %middle_3.1.e), channel_id=1, source_target_pairs={{0,32},{32,0},{64,96},{96,64},{128,160},{160,128},{192,224},{224,1... | collective-permute-start | bytes 30728 | tf_op jit(solution)/shard_map/ppermute | solution.py:296
  78.5 5.9 %collective-permute-start.27 = (f32[5,4,128]{2,1,0:T(4,128)S(1)}, f32[5,4,128]{2,1,0:T(4,128)S(1)}, u32[]{:S(2)}, u32[]{:S(2)}) collective-permute-start(f32[5,4,128]{2,1,0:T(4,128)S(1)} %middle_3.1.e), channel_id=1, source_target_pairs={{0,31},{1,0},{2,1},{3,2},{4,3},{5,4},{6,5},{7,6},{8,7},{9,8},{10,9... | collective-permute-start | bytes 30728 | tf_op jit(solution)/shard_map/ppermute | solution.py:292
  86.0 10.3 %collective-permute-start.30 = (f32[5,128]{1,0:T(8,128)S(1)}, f32[5,128]{1,0:T(8,128)S(1)}, u32[]{:S(2)}, u32[]{:S(2)}) collective-permute-start(f32[5,128]{1,0:T(8,128)S(1)} %get-tuple-element.56), channel_id=1, source_target_pairs={{0,30},{1,31},{2,0},{3,1},{4,2},{5,3},{6,4},{7,5},{8,6},{9,7},{10,... | collective-permute-start | bytes 7688 | tf_op jit(solution)/shard_map/ppermute | solution.py:292
  96.3 1.7 %collective-permute-start.32 = (f32[5,128]{1,0:T(8,128)S(1)}, f32[5,128]{1,0:T(8,128)S(1)}, u32[]{:S(2)}, u32[]{:S(2)}) collective-permute-start(f32[5,128]{1,0:T(8,128)S(1)} %get-tuple-element.58), channel_id=1, source_target_pairs={{0,1},{1,2},{2,3},{3,4},{4,5},{5,6},{6,7},{7,8},{8,9},{9,10},{10,1... | collective-permute-start | bytes 7688 | tf_op jit(solution)/shard_map/ppermute | solution.py:292
  99.3 4.5 %collective-permute-done.33.r0 = f32[5,128]{1,0:T(8,128)S(1)} collective-permute-done((f32[5,128]{1,0:T(8,128)S(1)}, f32[5,128]{1,0:T(8,128)S(1)}, u32[]{:S(2)}, u32[]{:S(2)}) %collective-permute-start.33) | collective-permute-done | bytes 2592 | tf_op jit(solution)/shard_map/ppermute | solution.py:292
  105.5 1.7 %collective-permute-start.36 = (f32[5,128]{1,0:T(8,128)S(1)}, f32[5,128]{1,0:T(8,128)S(1)}, u32[]{:S(2)}, u32[]{:S(2)}) collective-permute-start(f32[5,128]{1,0:T(8,128)S(1)} %get-tuple-element.63), channel_id=1, source_target_pairs={{0,1},{1,2},{2,3},{3,4},{4,5},{5,6},{6,7},{7,8},{8,9},{9,10},{10,1... | collective-permute-start | bytes 7688 | tf_op jit(solution)/shard_map/ppermute | solution.py:292
  108.6 4.4 %collective-permute-done.37.r0 = f32[5,128]{1,0:T(8,128)S(1)} collective-permute-done((f32[5,128]{1,0:T(8,128)S(1)}, f32[5,128]{1,0:T(8,128)S(1)}, u32[]{:S(2)}, u32[]{:S(2)}) %collective-permute-start.37) | collective-permute-done | bytes 2592 | tf_op jit(solution)/shard_map/ppermute | solution.py:292
  113.0 2.0 %fine_5.1 = f32[5,16,128]{2,1,0:T(8,128)} custom-call(f32[5,16,128]{2,1,0:T(8,128)S(1)} %get-tuple-element.60.x, f32[5,16,128]{2,1,0:T(8,128)S(1)} %bitcast.57, f32[5,5,16,128]{3,2,1,0:T(8,128)S(1)} %bitcast.37, f32[5,5,16,128]{3,2,1,0:T(8,128)S(1)} %bitcast.45, f32[6,5,5,16,128]{4,3,2,1,0:T(8,128)S(1)} %bitcast.32, s32[6,16,128]{2,1,0:T(8,128)S(1)} %bitcast.50, ...), custom_call_target="tpu_custom_call" | custom-call | tf_op jit(solution)/shard_map/fine_5/pallas_call | solution.py:279
  (114 shorter events, 31.9 us)
Async XLA Ops:
  2.9 7.6 %collective-permute-start = (f32[5,128]{1,0:T(8,128)S(1)}, f32[5,128]{1,0:T(8,128)S(1)}, u32[]{:S(2)}, u32[]{:S(2)}) collective-permute-start(f32[5,128]{1,0:T(8,128)S(1)} %get-tuple-element.37), channel_id=1, source_target_pairs={{0,30},{1,31},{2,0},{3,1},{4,2},{5,3},{6,4},{7,5},{8,6},{9,7},{10,... | collective-permute-start | bytes 7688 | tf_op jit(solution)/shard_map/ppermute | solution.py:292
  10.5 5.8 %collective-permute-start.3 = (f32[5,128]{1,0:T(8,128)S(1)}, f32[5,128]{1,0:T(8,128)S(1)}, u32[]{:S(2)}, u32[]{:S(2)}) collective-permute-start(f32[5,128]{1,0:T(8,128)S(1)} %get-tuple-element.40), channel_id=1, source_target_pairs={{0,2},{1,3},{2,4},{3,5},{4,6},{5,7},{6,8},{7,9},{8,10},{9,11},{10,... | collective-permute-start | bytes 7688 | tf_op jit(solution)/shard_map/ppermute | solution.py:292
  23.2 3.5 %collective-permute-start.5 = (f32[5,128]{1,0:T(8,128)S(1)}, f32[5,128]{1,0:T(8,128)S(1)}, u32[]{:S(2)}, u32[]{:S(2)}) collective-permute-start(f32[5,128]{1,0:T(8,128)S(1)} %get-tuple-element.43), channel_id=1, source_target_pairs={{0,31},{1,0},{2,1},{3,2},{4,3},{5,4},{6,5},{7,6},{8,7},{9,8},{10,9... | collective-permute-start | bytes 7688 | tf_op jit(solution)/shard_map/ppermute | solution.py:292
  25.1 5.8 %collective-permute-start.7 = (f32[5,128]{1,0:T(8,128)S(1)}, f32[5,128]{1,0:T(8,128)S(1)}, u32[]{:S(2)}, u32[]{:S(2)}) collective-permute-start(f32[5,128]{1,0:T(8,128)S(1)} %get-tuple-element.45), channel_id=1, source_target_pairs={{0,2},{1,3},{2,4},{3,5},{4,6},{5,7},{6,8},{7,9},{8,10},{9,11},{10,... | collective-permute-start | bytes 7688 | tf_op jit(solution)/shard_map/ppermute | solution.py:292
  32.5 3.3 %collective-permute-start.9 = (f32[5,128]{1,0:T(8,128)S(1)}, f32[5,128]{1,0:T(8,128)S(1)}, u32[]{:S(2)}, u32[]{:S(2)}) collective-permute-start(f32[5,128]{1,0:T(8,128)S(1)} %get-tuple-element.48), channel_id=1, source_target_pairs={{0,31},{1,0},{2,1},{3,2},{4,3},{5,4},{6,5},{7,6},{8,7},{9,8},{10,9... | collective-permute-start | bytes 7688 | tf_op jit(solution)/shard_map/ppermute | solution.py:292
  34.4 5.8 %collective-permute-start.11 = (f32[5,128]{1,0:T(8,128)S(1)}, f32[5,128]{1,0:T(8,128)S(1)}, u32[]{:S(2)}, u32[]{:S(2)}) collective-permute-start(f32[5,128]{1,0:T(8,128)S(1)} %get-tuple-element.50), channel_id=1, source_target_pairs={{0,2},{1,3},{2,4},{3,5},{4,6},{5,7},{6,8},{7,9},{8,10},{9,11},{10,... | collective-permute-start | bytes 7688 | tf_op jit(solution)/shard_map/ppermute | solution.py:292
  47.1 3.9 %collective-permute-start.17 = (f32[5,4,128]{2,1,0:T(4,128)S(1)}, f32[5,4,128]{2,1,0:T(4,128)S(1)}, u32[]{:S(2)}, u32[]{:S(2)}) collective-permute-start(f32[5,4,128]{2,1,0:T(4,128)S(1)} %middle_2.1.e), channel_id=1, source_target_pairs={{0,32},{32,0},{64,96},{96,64},{128,160},{160,128},{192,224},{224,1... | collective-permute-start | bytes 30728 | tf_op jit(solution)/shard_map/ppermute | solution.py:296
  47.4 4.2 %collective-permute-start.16 = (f32[5,4,128]{2,1,0:T(4,128)S(1)}, f32[5,4,128]{2,1,0:T(4,128)S(1)}, u32[]{:S(2)}, u32[]{:S(2)}) collective-permute-start(f32[5,4,128]{2,1,0:T(4,128)S(1)} %middle_2.1.e), channel_id=1, source_target_pairs={{0,1},{1,2},{2,3},{3,4},{4,5},{5,6},{6,7},{7,8},{8,9},{9,10},{10,1... | collective-permute-start | bytes 30728 | tf_op jit(solution)/shard_map/ppermute | solution.py:292
  47.7 4.2 %collective-permute-start.15 = (f32[5,4,128]{2,1,0:T(4,128)S(1)}, f32[5,4,128]{2,1,0:T(4,128)S(1)}, u32[]{:S(2)}, u32[]{:S(2)}) collective-permute-start(f32[5,4,128]{2,1,0:T(4,128)S(1)} %middle_2.1.e), channel_id=1, source_target_pairs={{0,31},{1,0},{2,1},{3,2},{4,3},{5,4},{6,5},{7,6},{8,7},{9,8},{10,9... | collective-permute-start | bytes 30728 | tf_op jit(solution)/shard_map/ppermute | solution.py:292
  52.5 4.7 %collective-permute-start.20 = (f32[5,128]{1,0:T(8,128)S(1)}, f32[5,128]{1,0:T(8,128)S(1)}, u32[]{:S(2)}, u32[]{:S(2)}) collective-permute-start(f32[5,128]{1,0:T(8,128)S(1)} %get-tuple-element.53.field), channel_id=1, source_target_pairs={{0,32},{32,0},{64,96},{96,64},{128,160},{160,128},{192,224},{224,1... | collective-permute-start | bytes 7688 | tf_op jit(solution)/shard_map/ppermute | solution.py:296
  54.1 4.0 %collective-permute-start.19 = (f32[5,128]{1,0:T(8,128)S(1)}, f32[5,128]{1,0:T(8,128)S(1)}, u32[]{:S(2)}, u32[]{:S(2)}) collective-permute-start(f32[5,128]{1,0:T(8,128)S(1)} %get-tuple-element.53.field), channel_id=1, source_target_pairs={{0,64},{32,96},{64,0},{96,32},{128,192},{160,224},{192,128},{224,1... | collective-permute-start | bytes 7688 | tf_op jit(solution)/shard_map/ppermute | solution.py:296
  57.1 4.3 %collective-permute-start.18 = (f32[5,128]{1,0:T(8,128)S(1)}, f32[5,128]{1,0:T(8,128)S(1)}, u32[]{:S(2)}, u32[]{:S(2)}) collective-permute-start(f32[5,128]{1,0:T(8,128)S(1)} %get-tuple-element.53.field), channel_id=1, source_target_pairs={{0,96},{32,64},{64,32},{96,0},{128,224},{160,192},{192,160},{224,1... | collective-permute-start | bytes 7688 | tf_op jit(solution)/shard_map/ppermute | solution.py:296
  61.5 3.6 %collective-permute-start.23 = (f32[5,128]{1,0:T(8,128)S(1)}, f32[5,128]{1,0:T(8,128)S(1)}, u32[]{:S(2)}, u32[]{:S(2)}) collective-permute-start(f32[5,128]{1,0:T(8,128)S(1)} %coarse_2.1.field), channel_id=1, source_target_pairs={{0,32},{32,0},{64,96},{96,64},{128,160},{160,128},{192,224},{224,1... | collective-permute-start | bytes 7688 | tf_op jit(solution)/shard_map/ppermute | solution.py:296
  61.6 3.5 %collective-permute-start.22 = (f32[5,128]{1,0:T(8,128)S(1)}, f32[5,128]{1,0:T(8,128)S(1)}, u32[]{:S(2)}, u32[]{:S(2)}) collective-permute-start(f32[5,128]{1,0:T(8,128)S(1)} %coarse_2.1.field), channel_id=1, source_target_pairs={{0,64},{32,96},{64,0},{96,32},{128,192},{160,224},{192,128},{224,1... | collective-permute-start | bytes 7688 | tf_op jit(solution)/shard_map/ppermute | solution.py:296
  61.9 4.3 %collective-permute-start.21 = (f32[5,128]{1,0:T(8,128)S(1)}, f32[5,128]{1,0:T(8,128)S(1)}, u32[]{:S(2)}, u32[]{:S(2)}) collective-permute-start(f32[5,128]{1,0:T(8,128)S(1)} %coarse_2.1.field), channel_id=1, source_target_pairs={{0,96},{32,64},{64,32},{96,0},{128,224},{160,192},{192,160},{224,1... | collective-permute-start | bytes 7688 | tf_op jit(solution)/shard_map/ppermute | solution.py:296
  66.4 9.3 %collective-permute-start.26 = (f32[5,4,128]{2,1,0:T(4,128)S(1)}, f32[5,4,128]{2,1,0:T(4,128)S(1)}, u32[]{:S(2)}, u32[]{:S(2)}) collective-permute-start(f32[5,4,128]{2,1,0:T(4,128)S(1)} %coarse_3.1.e), channel_id=1, source_target_pairs={{0,32},{32,0},{64,96},{96,64},{128,160},{160,128},{192,224},{224,1... | collective-permute-start | bytes 30728 | tf_op jit(solution)/shard_map/ppermute | solution.py:296
  66.7 9.7 %collective-permute-start.25 = (f32[5,4,128]{2,1,0:T(4,128)S(1)}, f32[5,4,128]{2,1,0:T(4,128)S(1)}, u32[]{:S(2)}, u32[]{:S(2)}) collective-permute-start(f32[5,4,128]{2,1,0:T(4,128)S(1)} %coarse_3.1.e), channel_id=1, source_target_pairs={{0,1},{1,2},{2,3},{3,4},{4,5},{5,6},{6,7},{7,8},{8,9},{9,10},{10,1... | collective-permute-start | bytes 30728 | tf_op jit(solution)/shard_map/ppermute | solution.py:292
  68.7 7.8 %collective-permute-start.24 = (f32[5,4,128]{2,1,0:T(4,128)S(1)}, f32[5,4,128]{2,1,0:T(4,128)S(1)}, u32[]{:S(2)}, u32[]{:S(2)}) collective-permute-start(f32[5,4,128]{2,1,0:T(4,128)S(1)} %coarse_3.1.e), channel_id=1, source_target_pairs={{0,31},{1,0},{2,1},{3,2},{4,3},{5,4},{6,5},{7,6},{8,7},{9,8},{10,9... | collective-permute-start | bytes 30728 | tf_op jit(solution)/shard_map/ppermute | solution.py:292
  77.0 7.4 %collective-permute-start.29 = (f32[5,4,128]{2,1,0:T(4,128)S(1)}, f32[5,4,128]{2,1,0:T(4,128)S(1)}, u32[]{:S(2)}, u32[]{:S(2)}) collective-permute-start(f32[5,4,128]{2,1,0:T(4,128)S(1)} %middle_3.1.e), channel_id=1, source_target_pairs={{0,32},{32,0},{64,96},{96,64},{128,160},{160,128},{192,224},{224,1... | collective-permute-start | bytes 30728 | tf_op jit(solution)/shard_map/ppermute | solution.py:296
  78.5 6.6 %collective-permute-start.28 = (f32[5,4,128]{2,1,0:T(4,128)S(1)}, f32[5,4,128]{2,1,0:T(4,128)S(1)}, u32[]{:S(2)}, u32[]{:S(2)}) collective-permute-start(f32[5,4,128]{2,1,0:T(4,128)S(1)} %middle_3.1.e), channel_id=1, source_target_pairs={{0,1},{1,2},{2,3},{3,4},{4,5},{5,6},{6,7},{7,8},{8,9},{9,10},{10,1... | collective-permute-start | bytes 30728 | tf_op jit(solution)/shard_map/ppermute | solution.py:292
  78.5 6.7 %collective-permute-start.27 = (f32[5,4,128]{2,1,0:T(4,128)S(1)}, f32[5,4,128]{2,1,0:T(4,128)S(1)}, u32[]{:S(2)}, u32[]{:S(2)}) collective-permute-start(f32[5,4,128]{2,1,0:T(4,128)S(1)} %middle_3.1.e), channel_id=1, source_target_pairs={{0,31},{1,0},{2,1},{3,2},{4,3},{5,4},{6,5},{7,6},{8,7},{9,8},{10,9... | collective-permute-start | bytes 30728 | tf_op jit(solution)/shard_map/ppermute | solution.py:292
  86.0 12.1 %collective-permute-start.30 = (f32[5,128]{1,0:T(8,128)S(1)}, f32[5,128]{1,0:T(8,128)S(1)}, u32[]{:S(2)}, u32[]{:S(2)}) collective-permute-start(f32[5,128]{1,0:T(8,128)S(1)} %get-tuple-element.56), channel_id=1, source_target_pairs={{0,30},{1,31},{2,0},{3,1},{4,2},{5,3},{6,4},{7,5},{8,6},{9,7},{10,... | collective-permute-start | bytes 7688 | tf_op jit(solution)/shard_map/ppermute | solution.py:292
  98.0 5.8 %collective-permute-start.33 = (f32[5,128]{1,0:T(8,128)S(1)}, f32[5,128]{1,0:T(8,128)S(1)}, u32[]{:S(2)}, u32[]{:S(2)}) collective-permute-start(f32[5,128]{1,0:T(8,128)S(1)} %get-tuple-element.59), channel_id=1, source_target_pairs={{0,2},{1,3},{2,4},{3,5},{4,6},{5,7},{6,8},{7,9},{8,10},{9,11},{10,... | collective-permute-start | bytes 7688 | tf_op jit(solution)/shard_map/ppermute | solution.py:292
  107.2 5.8 %collective-permute-start.37 = (f32[5,128]{1,0:T(8,128)S(1)}, f32[5,128]{1,0:T(8,128)S(1)}, u32[]{:S(2)}, u32[]{:S(2)}) collective-permute-start(f32[5,128]{1,0:T(8,128)S(1)} %get-tuple-element.64), channel_id=1, source_target_pairs={{0,2},{1,3},{2,4},{3,5},{4,6},{5,7},{6,8},{7,9},{8,10},{9,11},{10,... | collective-permute-start | bytes 7688 | tf_op jit(solution)/shard_map/ppermute | solution.py:292
  (37 other events, 379.5 us)

commit v2 on v1

--- a/solution.py
+++ b/solution.py
@@ -132,15 +132,29 @@
             outs[j][k : k + 1, :] = picked[j : j + 1, :]
 
 
-def send_kernel(x, send, count, s0, s1, s2, s3, where, live):
+def send_kernel(
+    send_far, count_far, x_far, b_far, diag_far, inverse_far, coupling_far, columns_far,
+    s0, s1, s2, s3, where, live, x, b, diag, inverse, coupling, columns, send, count, done
+):
+    pairs = (
+        (send_far, send), (count_far, count), (x_far, x), (columns_far, columns), (b_far, b),
+        (diag_far, diag), (inverse_far, inverse), (coupling_far, coupling),
+    )
+    copies = [pltpu.make_async_copy(a, z, done.at[i]) for i, (a, z) in enumerate(pairs)]
+    for copy in copies:
+        copy.start()
+    for copy in copies[:3]:
+        copy.wait()
     lane = lax.broadcasted_iota(jnp.int32, (1, LANES), 1)
     for j in range(4):
         first = SLOT_ROWS * ((3 - j) % 2)
         row = send[j : j + 1, :]
         where[j : j + 1, :] = jnp.concatenate([row, row], axis=1)
-        inside = (lane >= first) & (lane < first + count[j])
-        live[j : j + 1, :] = jnp.where(inside, 1.0, 0.0)
+        end = jnp.broadcast_to(count[0:1, j : j + 1], (1, LANES)) + first
+        live[j : j + 1, :] = jnp.where((lane >= first) & (lane < end), 1.0, 0.0)
     pack_sends(x, where, live, (s0, s1, s2, s3))
+    for copy in copies[3:]:
+        copy.wait()
 
 
 def fine_kernel(last, x, b, diag, inverse, coupling, columns, where, live, r3, r2, r1, r0, *rest):
@@ -272,15 +286,14 @@
 
 
 VMEM = pl.BlockSpec(memory_space=pltpu.VMEM)
-SMEM = pl.BlockSpec(memory_space=pltpu.SMEM)
-
-
-def call(name, kernel, args, shapes, scratch=(), scalars=()):
+
+
+def call(name, kernel, args, shapes, scratch=()):
     return pl.pallas_call(
         kernel,
         name=name,
-        out_shape=[s if isinstance(s, jax.ShapeDtypeStruct) else jax.ShapeDtypeStruct(s, F32) for s in shapes],
-        in_specs=[SMEM if i in scalars else VMEM for i in range(len(args))],
+        out_shape=[jax.ShapeDtypeStruct(s, F32) for s in shapes],
+        in_specs=[VMEM] * len(args),
         out_specs=[VMEM] * len(shapes),
         scratch_shapes=[pltpu.VMEM(s, F32) for s in scratch],
         compiler_params=pltpu.CompilerParams(vmem_limit_bytes=16 * 1024 * 1024),
@@ -306,7 +319,7 @@
 
     b, x = dense(right_side), dense(initial_guess)
     f_mats = tuple(map(dense, (fine_diag, fine_inverse, fine_coupling, fine_columns)))
-    f_send, f_count, f_aggregate = fine_send[0, 0], fine_count[0, 0], dense(fine_aggregate)
+    f_send, f_count, f_aggregate = fine_send[0, 0], fine_count[0], dense(fine_aggregate)
     m_mats = tuple(map(dense, (middle_diag, middle_inverse, middle_coupling, middle_columns)))
     m_aggregate = dense(middle_aggregate)
     c_mats = (coarse_diag[0, 0], coarse_inverse[0, 0], coarse_coupling[0, 0], coarse_columns[0, 0])
@@ -327,10 +340,26 @@
     def coarse_exchange(c):
         return [group_swap(c, mask) for mask in (3, 2, 1)]
 
-    *sends, where, live = call(
-        "send", send_kernel, (x, f_send, f_count),
-        slots + [jax.ShapeDtypeStruct((4, LANES), jnp.int32), (4, LANES)], scalars=(2,),
-    )
+    def shape_of(array):
+        return jax.ShapeDtypeStruct(array.shape, array.dtype)
+
+    far = (f_send, f_count, x, b) + f_mats
+    out = pl.pallas_call(
+        send_kernel,
+        name="send",
+        out_shape=[jax.ShapeDtypeStruct((5, LANES), F32)] * 4
+        + [jax.ShapeDtypeStruct((4, LANES), jnp.int32), jax.ShapeDtypeStruct((4, LANES), F32)]
+        + [shape_of(array) for array in far[2:]],
+        in_specs=[pl.BlockSpec(memory_space=pltpu.HBM)] * len(far),
+        out_specs=[VMEM] * 12,
+        scratch_shapes=[
+            pltpu.VMEM(f_send.shape, jnp.int32),
+            pltpu.VMEM(f_count.shape, jnp.int32),
+            pltpu.SemaphoreType.DMA((8,)),
+        ],
+        compiler_params=pltpu.CompilerParams(vmem_limit_bytes=16 * 1024 * 1024),
+    )(*(pltpu.with_memory_space_constraint(array, pltpu.HBM) for array in far))
+    sends, (where, live, x, b), f_mats = out[:4], out[4:8], tuple(out[8:])
 
     def fine_sweep(name, x, sends, last=False):
         out = call(

time: 115 us -> 108 us (0.939)
  local copies, waits for them, and re-layouts: 6.94 us -> 0.08 us
  waiting for transfers between devices: 35.7 us -> 32.6 us
  starting transfers between devices: 60.7 us -> 62.6 us
    unnamed x49 -> x23, local copies, waits for them, and re-layouts: 6.93 us -> 0.07 us
    ppermute x28, waiting for transfers between devices: 29.9 us -> 26.4 us  [passed_along(): return lax.ppermute(x, 'dom', [(i, (i + by) % size) for i in range(size)])]
    ppermute x10, starting transfers between devices: 12.1 us -> 15 us  [group_swap(): lax.ppermute(x, 'grp', [(i, i ^ mask) for i in range(lax.axis_size('grp'))])]
  transfers between devices with their start and end apart: 38 -> 38, of which waited for: 21 -> 19; matrix products, arithmetic and copies ran while one was open for 0% -> 0% of each run, Pallas kernels for 0% -> 0%
where the time goes in v2:
time: 108 us
  starting transfers between devices  62.6 us (58%)
  waiting for transfers between devices  32.6 us (30%)
  Pallas kernels  12.2 us (11%)
    ppermute x28, starting transfers between devices, passed_along(): return lax.ppermute(x, 'dom', [(i, (i + by) % size) for i in range(size)])  47.7 us
    ppermute x28, waiting for transfers between devices, passed_along(): return lax.ppermute(x, 'dom', [(i, (i + by) % size) for i in range(size)])  26.4 us
    ppermute x10, starting transfers between devices, group_swap(): lax.ppermute(x, 'grp', [(i, i ^ mask) for i in range(lax.axis_size('grp'))])  15 us
    pallas_call x11, Pallas kernels, call(): pl.pallas_call(kernel, name=name, out_shape=[jax.ShapeDtypeStruct(s, F32)...  10.5 us
    ppermute x10, waiting for transfers between devices, group_swap(): lax.ppermute(x, 'grp', [(i, i ^ mask) for i in range(lax.axis_size('grp'))])  6.2 us
  transfers between devices with their start and end apart: 38, of which 19 were waited for; matrix products, arithmetic and copies ran while one was open for 0% of the time, Pallas kernels for 0%

profile of v2, /device:TPU:1, one launch (start us, length us, event | category | flops | bytes accessed | tf_op | source)
XLA Modules:
  0.0 107.7 jit_solution(3273402498963984341)
XLA Ops:
  0.0 1.7 %send.1 = (f32[5,128]{1,0:T(8,128)S(1)}, f32[5,128]{1,0:T(8,128)S(1)}, f32[5,128]{1,0:T(8,128)S(1)}, f32[5,128]{1,0:T(8,128)S(1)}, s32[4,128]{1,0:T(4,128)S(1)},...) custom-call(s32[4,64]{1,0:T(4,128)} %bitcast.63, ...), custom_call_target="tpu_custom_call" | custom-call | tf_op jit(solution)/shard_map/send/pallas_call | solution.py:347
  1.7 5.8 %collective-permute-start = (f32[5,128]{1,0:T(8,128)S(1)}, f32[5,128]{1,0:T(8,128)S(1)}, u32[]{:S(2)}, u32[]{:S(2)}) collective-permute-start(f32[5,128]{1,0:T(8,128)S(1)} %get-tuple-element.49), channel_id=1, source_target_pairs={{0,30},{1,31},{2,0},{3,1},{4,2},{5,3},{6,4},{7,5},{8,6},{9,7},{10,... | collective-permute-start | bytes 7688 | tf_op jit(solution)/shard_map/ppermute | solution.py:305
  10.5 4.5 %collective-permute-done.3.r0 = f32[5,128]{1,0:T(8,128)S(1)} collective-permute-done((f32[5,128]{1,0:T(8,128)S(1)}, f32[5,128]{1,0:T(8,128)S(1)}, u32[]{:S(2)}, u32[]{:S(2)}) %collective-permute-start.3) | collective-permute-done | bytes 2592 | tf_op jit(solution)/shard_map/ppermute | solution.py:305
  20.7 4.2 %collective-permute-done.7.r0 = f32[5,128]{1,0:T(8,128)S(1)} collective-permute-done((f32[5,128]{1,0:T(8,128)S(1)}, f32[5,128]{1,0:T(8,128)S(1)}, u32[]{:S(2)}, u32[]{:S(2)}) %collective-permute-start.7) | collective-permute-done | bytes 2592 | tf_op jit(solution)/shard_map/ppermute | solution.py:305
  26.7 4.8 %collective-permute-start.8 = (f32[5,128]{1,0:T(8,128)S(1)}, f32[5,128]{1,0:T(8,128)S(1)}, u32[]{:S(2)}, u32[]{:S(2)}) collective-permute-start(f32[5,128]{1,0:T(8,128)S(1)} %get-tuple-element.59), channel_id=1, source_target_pairs={{0,30},{1,31},{2,0},{3,1},{4,2},{5,3},{6,4},{7,5},{8,6},{9,7},{10,... | collective-permute-start | bytes 7688 | tf_op jit(solution)/shard_map/ppermute | solution.py:305
  32.6 1.8 %collective-permute-done.9.r2 = f32[5,128]{1,0:T(8,128)S(1)} collective-permute-done((f32[5,128]{1,0:T(8,128)S(1)}, f32[5,128]{1,0:T(8,128)S(1)}, u32[]{:S(2)}, u32[]{:S(2)}) %collective-permute-start.9) | collective-permute-done | bytes 2592 | tf_op jit(solution)/shard_map/ppermute | solution.py:305
  36.3 1.7 %collective-permute-start.13 = (f32[5,4,128]{2,1,0:T(4,128)S(1)}, f32[5,4,128]{2,1,0:T(4,128)S(1)}, u32[]{:S(2)}, u32[]{:S(2)}) collective-permute-start(f32[5,4,128]{2,1,0:T(4,128)S(1)} %get-tuple-element.63.e), channel_id=1, source_target_pairs={{0,1},{1,2},{2,3},{3,4},{4,5},{5,6},{6,7},{7,8},{8,9},{9,10},{10,1... | collective-permute-start | bytes 30728 | tf_op jit(solution)/shard_map/ppermute | solution.py:305
  37.9 1.6 %collective-permute-start.14 = (f32[5,4,128]{2,1,0:T(4,128)S(1)}, f32[5,4,128]{2,1,0:T(4,128)S(1)}, u32[]{:S(2)}, u32[]{:S(2)}) collective-permute-start(f32[5,4,128]{2,1,0:T(4,128)S(1)} %get-tuple-element.63.e), channel_id=1, source_target_pairs={{0,32},{32,0},{64,96},{96,64},{128,160},{160,128},{192,224},{224,1... | collective-permute-start | bytes 30728 | tf_op jit(solution)/shard_map/ppermute | solution.py:309
  39.6 2.4 %collective-permute-done.13.left = f32[5,4,128]{2,1,0:T(4,128)S(1)} collective-permute-done((f32[5,4,128]{2,1,0:T(4,128)S(1)}, f32[5,4,128]{2,1,0:T(4,128)S(1)}, u32[]{:S(2)}, u32[]{:S(2)}) %collective-permute-start.13) | collective-permute-done | bytes 10272 | tf_op jit(solution)/shard_map/ppermute | solution.py:305
  42.4 5.8 %collective-permute-start.15 = (f32[5,4,128]{2,1,0:T(4,128)S(1)}, f32[5,4,128]{2,1,0:T(4,128)S(1)}, u32[]{:S(2)}, u32[]{:S(2)}) collective-permute-start(f32[5,4,128]{2,1,0:T(4,128)S(1)} %middle_2.1.e), channel_id=1, source_target_pairs={{0,31},{1,0},{2,1},{3,2},{4,3},{5,4},{6,5},{7,6},{8,7},{9,8},{10,9... | collective-permute-start | bytes 30728 | tf_op jit(solution)/shard_map/ppermute | solution.py:305
  48.3 1.6 %collective-permute-start.17 = (f32[5,4,128]{2,1,0:T(4,128)S(1)}, f32[5,4,128]{2,1,0:T(4,128)S(1)}, u32[]{:S(2)}, u32[]{:S(2)}) collective-permute-start(f32[5,4,128]{2,1,0:T(4,128)S(1)} %middle_2.1.e), channel_id=1, source_target_pairs={{0,32},{32,0},{64,96},{96,64},{128,160},{160,128},{192,224},{224,1... | collective-permute-start | bytes 30728 | tf_op jit(solution)/shard_map/ppermute | solution.py:309
  51.5 4.3 %collective-permute-start.18 = (f32[5,128]{1,0:T(8,128)S(1)}, f32[5,128]{1,0:T(8,128)S(1)}, u32[]{:S(2)}, u32[]{:S(2)}) collective-permute-start(f32[5,128]{1,0:T(8,128)S(1)} %get-tuple-element.65.field), channel_id=1, source_target_pairs={{0,96},{32,64},{64,32},{96,0},{128,224},{160,192},{192,160},{224,1... | collective-permute-start | bytes 7688 | tf_op jit(solution)/shard_map/ppermute | solution.py:309
  56.8 2.4 %collective-permute-done.19.p2 = f32[5,128]{1,0:T(8,128)S(1)} collective-permute-done((f32[5,128]{1,0:T(8,128)S(1)}, f32[5,128]{1,0:T(8,128)S(1)}, u32[]{:S(2)}, u32[]{:S(2)}) %collective-permute-start.19) | collective-permute-done | bytes 2592 | tf_op jit(solution)/shard_map/ppermute | solution.py:309
  60.9 2.0 %collective-permute-start.23 = (f32[5,128]{1,0:T(8,128)S(1)}, f32[5,128]{1,0:T(8,128)S(1)}, u32[]{:S(2)}, u32[]{:S(2)}) collective-permute-start(f32[5,128]{1,0:T(8,128)S(1)} %coarse_2.1.field), channel_id=1, source_target_pairs={{0,32},{32,0},{64,96},{96,64},{128,160},{160,128},{192,224},{224,1... | collective-permute-start | bytes 7688 | tf_op jit(solution)/shard_map/ppermute | solution.py:309
  64.2 7.9 %collective-permute-start.24 = (f32[5,4,128]{2,1,0:T(4,128)S(1)}, f32[5,4,128]{2,1,0:T(4,128)S(1)}, u32[]{:S(2)}, u32[]{:S(2)}) collective-permute-start(f32[5,4,128]{2,1,0:T(4,128)S(1)} %coarse_3.1.e), channel_id=1, source_target_pairs={{0,31},{1,0},{2,1},{3,2},{4,3},{5,4},{6,5},{7,6},{8,7},{9,8},{10,9... | collective-permute-start | bytes 30728 | tf_op jit(solution)/shard_map/ppermute | solution.py:305
  72.1 1.7 %collective-permute-start.26 = (f32[5,4,128]{2,1,0:T(4,128)S(1)}, f32[5,4,128]{2,1,0:T(4,128)S(1)}, u32[]{:S(2)}, u32[]{:S(2)}) collective-permute-start(f32[5,4,128]{2,1,0:T(4,128)S(1)} %coarse_3.1.e), channel_id=1, source_target_pairs={{0,32},{32,0},{64,96},{96,64},{128,160},{160,128},{192,224},{224,1... | collective-permute-start | bytes 30728 | tf_op jit(solution)/shard_map/ppermute | solution.py:309
  75.3 4.0 %collective-permute-start.27 = (f32[5,4,128]{2,1,0:T(4,128)S(1)}, f32[5,4,128]{2,1,0:T(4,128)S(1)}, u32[]{:S(2)}, u32[]{:S(2)}) collective-permute-start(f32[5,4,128]{2,1,0:T(4,128)S(1)} %middle_3.1.e), channel_id=1, source_target_pairs={{0,31},{1,0},{2,1},{3,2},{4,3},{5,4},{6,5},{7,6},{8,7},{9,8},{10,9... | collective-permute-start | bytes 30728 | tf_op jit(solution)/shard_map/ppermute | solution.py:305
  79.4 1.7 %collective-permute-start.29 = (f32[5,4,128]{2,1,0:T(4,128)S(1)}, f32[5,4,128]{2,1,0:T(4,128)S(1)}, u32[]{:S(2)}, u32[]{:S(2)}) collective-permute-start(f32[5,4,128]{2,1,0:T(4,128)S(1)} %middle_3.1.e), channel_id=1, source_target_pairs={{0,32},{32,0},{64,96},{96,64},{128,160},{160,128},{192,224},{224,1... | collective-permute-start | bytes 30728 | tf_op jit(solution)/shard_map/ppermute | solution.py:309
  82.9 6.2 %collective-permute-start.30 = (f32[5,128]{1,0:T(8,128)S(1)}, f32[5,128]{1,0:T(8,128)S(1)}, u32[]{:S(2)}, u32[]{:S(2)}) collective-permute-start(f32[5,128]{1,0:T(8,128)S(1)} %get-tuple-element.68), channel_id=1, source_target_pairs={{0,30},{1,31},{2,0},{3,1},{4,2},{5,3},{6,4},{7,5},{8,6},{9,7},{10,... | collective-permute-start | bytes 7688 | tf_op jit(solution)/shard_map/ppermute | solution.py:305
  89.1 1.7 %collective-permute-start.32 = (f32[5,128]{1,0:T(8,128)S(1)}, f32[5,128]{1,0:T(8,128)S(1)}, u32[]{:S(2)}, u32[]{:S(2)}) collective-permute-start(f32[5,128]{1,0:T(8,128)S(1)} %get-tuple-element.70), channel_id=1, source_target_pairs={{0,1},{1,2},{2,3},{3,4},{4,5},{5,6},{6,7},{7,8},{8,9},{9,10},{10,1... | collective-permute-start | bytes 7688 | tf_op jit(solution)/shard_map/ppermute | solution.py:305
  92.1 4.5 %collective-permute-done.33.r0 = f32[5,128]{1,0:T(8,128)S(1)} collective-permute-done((f32[5,128]{1,0:T(8,128)S(1)}, f32[5,128]{1,0:T(8,128)S(1)}, u32[]{:S(2)}, u32[]{:S(2)}) %collective-permute-start.33) | collective-permute-done | bytes 2592 | tf_op jit(solution)/shard_map/ppermute | solution.py:305
  98.3 1.7 %collective-permute-start.36 = (f32[5,128]{1,0:T(8,128)S(1)}, f32[5,128]{1,0:T(8,128)S(1)}, u32[]{:S(2)}, u32[]{:S(2)}) collective-permute-start(f32[5,128]{1,0:T(8,128)S(1)} %get-tuple-element.75), channel_id=1, source_target_pairs={{0,1},{1,2},{2,3},{3,4},{4,5},{5,6},{6,7},{7,8},{8,9},{9,10},{10,1... | collective-permute-start | bytes 7688 | tf_op jit(solution)/shard_map/ppermute | solution.py:305
  101.4 4.4 %collective-permute-done.37.r0 = f32[5,128]{1,0:T(8,128)S(1)} collective-permute-done((f32[5,128]{1,0:T(8,128)S(1)}, f32[5,128]{1,0:T(8,128)S(1)}, u32[]{:S(2)}, u32[]{:S(2)}) %collective-permute-start.37) | collective-permute-done | bytes 2592 | tf_op jit(solution)/shard_map/ppermute | solution.py:305
  105.8 2.0 %fine_5.1 = f32[5,16,128]{2,1,0:T(8,128)} custom-call(f32[5,16,128]{2,1,0:T(8,128)S(1)} %get-tuple-element.72.x, f32[5,16,128]{2,1,0:T(8,128)S(1)} %get-tuple-element.42.b, f32[5,5,16,128]{3,2,1,0:T(8,128)S(1)} %get-tuple-element.43.diag, f32[5,5,16,128]{3,2,1,0:T(8,128)S(1)} %get-tuple-element.44.inverse, ...), custom_call_target="tpu_custom_call" | custom-call | tf_op jit(solution)/shard_map/fine_5/pallas_call | solution.py:292
  (88 shorter events, 27.0 us)
Async XLA Ops:
  1.7 7.6 %collective-permute-start = (f32[5,128]{1,0:T(8,128)S(1)}, f32[5,128]{1,0:T(8,128)S(1)}, u32[]{:S(2)}, u32[]{:S(2)}) collective-permute-start(f32[5,128]{1,0:T(8,128)S(1)} %get-tuple-element.49), channel_id=1, source_target_pairs={{0,30},{1,31},{2,0},{3,1},{4,2},{5,3},{6,4},{7,5},{8,6},{9,7},{10,... | collective-permute-start | bytes 7688 | tf_op jit(solution)/shard_map/ppermute | solution.py:305
  9.3 5.8 %collective-permute-start.3 = (f32[5,128]{1,0:T(8,128)S(1)}, f32[5,128]{1,0:T(8,128)S(1)}, u32[]{:S(2)}, u32[]{:S(2)}) collective-permute-start(f32[5,128]{1,0:T(8,128)S(1)} %get-tuple-element.52), channel_id=1, source_target_pairs={{0,2},{1,3},{2,4},{3,5},{4,6},{5,7},{6,8},{7,9},{8,10},{9,11},{10,... | collective-permute-start | bytes 7688 | tf_op jit(solution)/shard_map/ppermute | solution.py:305
  16.6 3.3 %collective-permute-start.4 = (f32[5,128]{1,0:T(8,128)S(1)}, f32[5,128]{1,0:T(8,128)S(1)}, u32[]{:S(2)}, u32[]{:S(2)}) collective-permute-start(f32[5,128]{1,0:T(8,128)S(1)} %get-tuple-element.54), channel_id=1, source_target_pairs={{0,30},{1,31},{2,0},{3,1},{4,2},{5,3},{6,4},{7,5},{8,6},{9,7},{10,... | collective-permute-start | bytes 7688 | tf_op jit(solution)/shard_map/ppermute | solution.py:305
  17.2 3.5 %collective-permute-start.5 = (f32[5,128]{1,0:T(8,128)S(1)}, f32[5,128]{1,0:T(8,128)S(1)}, u32[]{:S(2)}, u32[]{:S(2)}) collective-permute-start(f32[5,128]{1,0:T(8,128)S(1)} %get-tuple-element.55), channel_id=1, source_target_pairs={{0,31},{1,0},{2,1},{3,2},{4,3},{5,4},{6,5},{7,6},{8,7},{9,8},{10,9... | collective-permute-start | bytes 7688 | tf_op jit(solution)/shard_map/ppermute | solution.py:305
  19.1 5.8 %collective-permute-start.7 = (f32[5,128]{1,0:T(8,128)S(1)}, f32[5,128]{1,0:T(8,128)S(1)}, u32[]{:S(2)}, u32[]{:S(2)}) collective-permute-start(f32[5,128]{1,0:T(8,128)S(1)} %get-tuple-element.57), channel_id=1, source_target_pairs={{0,2},{1,3},{2,4},{3,5},{4,6},{5,7},{6,8},{7,9},{8,10},{9,11},{10,... | collective-permute-start | bytes 7688 | tf_op jit(solution)/shard_map/ppermute | solution.py:305
  26.5 5.9 %collective-permute-start.10 = (f32[5,128]{1,0:T(8,128)S(1)}, f32[5,128]{1,0:T(8,128)S(1)}, u32[]{:S(2)}, u32[]{:S(2)}) collective-permute-start(f32[5,128]{1,0:T(8,128)S(1)} %get-tuple-element.61), channel_id=1, source_target_pairs={{0,1},{1,2},{2,3},{3,4},{4,5},{5,6},{6,7},{7,8},{8,9},{9,10},{10,1... | collective-permute-start | bytes 7688 | tf_op jit(solution)/shard_map/ppermute | solution.py:305
  26.6 6.1 %collective-permute-start.11 = (f32[5,128]{1,0:T(8,128)S(1)}, f32[5,128]{1,0:T(8,128)S(1)}, u32[]{:S(2)}, u32[]{:S(2)}) collective-permute-start(f32[5,128]{1,0:T(8,128)S(1)} %get-tuple-element.62), channel_id=1, source_target_pairs={{0,2},{1,3},{2,4},{3,5},{4,6},{5,7},{6,8},{7,9},{8,10},{9,11},{10,... | collective-permute-start | bytes 7688 | tf_op jit(solution)/shard_map/ppermute | solution.py:305
  26.7 6.0 %collective-permute-start.8 = (f32[5,128]{1,0:T(8,128)S(1)}, f32[5,128]{1,0:T(8,128)S(1)}, u32[]{:S(2)}, u32[]{:S(2)}) collective-permute-start(f32[5,128]{1,0:T(8,128)S(1)} %get-tuple-element.59), channel_id=1, source_target_pairs={{0,30},{1,31},{2,0},{3,1},{4,2},{5,3},{6,4},{7,5},{8,6},{9,7},{10,... | collective-permute-start | bytes 7688 | tf_op jit(solution)/shard_map/ppermute | solution.py:305
  36.1 3.5 %collective-permute-start.12 = (f32[5,4,128]{2,1,0:T(4,128)S(1)}, f32[5,4,128]{2,1,0:T(4,128)S(1)}, u32[]{:S(2)}, u32[]{:S(2)}) collective-permute-start(f32[5,4,128]{2,1,0:T(4,128)S(1)} %get-tuple-element.63.e), channel_id=1, source_target_pairs={{0,31},{1,0},{2,1},{3,2},{4,3},{5,4},{6,5},{7,6},{8,7},{9,8},{10,9... | collective-permute-start | bytes 30728 | tf_op jit(solution)/shard_map/ppermute | solution.py:305
  36.3 5.7 %collective-permute-start.13 = (f32[5,4,128]{2,1,0:T(4,128)S(1)}, f32[5,4,128]{2,1,0:T(4,128)S(1)}, u32[]{:S(2)}, u32[]{:S(2)}) collective-permute-start(f32[5,4,128]{2,1,0:T(4,128)S(1)} %get-tuple-element.63.e), channel_id=1, source_target_pairs={{0,1},{1,2},{2,3},{3,4},{4,5},{5,6},{6,7},{7,8},{8,9},{9,10},{10,1... | collective-permute-start | bytes 30728 | tf_op jit(solution)/shard_map/ppermute | solution.py:305
  37.9 4.0 %collective-permute-start.14 = (f32[5,4,128]{2,1,0:T(4,128)S(1)}, f32[5,4,128]{2,1,0:T(4,128)S(1)}, u32[]{:S(2)}, u32[]{:S(2)}) collective-permute-start(f32[5,4,128]{2,1,0:T(4,128)S(1)} %get-tuple-element.63.e), channel_id=1, source_target_pairs={{0,32},{32,0},{64,96},{96,64},{128,160},{160,128},{192,224},{224,1... | collective-permute-start | bytes 30728 | tf_op jit(solution)/shard_map/ppermute | solution.py:309
  42.4 7.5 %collective-permute-start.15 = (f32[5,4,128]{2,1,0:T(4,128)S(1)}, f32[5,4,128]{2,1,0:T(4,128)S(1)}, u32[]{:S(2)}, u32[]{:S(2)}) collective-permute-start(f32[5,4,128]{2,1,0:T(4,128)S(1)} %middle_2.1.e), channel_id=1, source_target_pairs={{0,31},{1,0},{2,1},{3,2},{4,3},{5,4},{6,5},{7,6},{8,7},{9,8},{10,9... | collective-permute-start | bytes 30728 | tf_op jit(solution)/shard_map/ppermute | solution.py:305
  51.5 5.3 %collective-permute-start.18 = (f32[5,128]{1,0:T(8,128)S(1)}, f32[5,128]{1,0:T(8,128)S(1)}, u32[]{:S(2)}, u32[]{:S(2)}) collective-permute-start(f32[5,128]{1,0:T(8,128)S(1)} %get-tuple-element.65.field), channel_id=1, source_target_pairs={{0,96},{32,64},{64,32},{96,0},{128,224},{160,192},{192,160},{224,1... | collective-permute-start | bytes 7688 | tf_op jit(solution)/shard_map/ppermute | solution.py:309
  55.8 3.4 %collective-permute-start.19 = (f32[5,128]{1,0:T(8,128)S(1)}, f32[5,128]{1,0:T(8,128)S(1)}, u32[]{:S(2)}, u32[]{:S(2)}) collective-permute-start(f32[5,128]{1,0:T(8,128)S(1)} %get-tuple-element.65.field), channel_id=1, source_target_pairs={{0,64},{32,96},{64,0},{96,32},{128,192},{160,224},{192,128},{224,1... | collective-permute-start | bytes 7688 | tf_op jit(solution)/shard_map/ppermute | solution.py:309
  55.8 3.4 %collective-permute-start.20 = (f32[5,128]{1,0:T(8,128)S(1)}, f32[5,128]{1,0:T(8,128)S(1)}, u32[]{:S(2)}, u32[]{:S(2)}) collective-permute-start(f32[5,128]{1,0:T(8,128)S(1)} %get-tuple-element.65.field), channel_id=1, source_target_pairs={{0,32},{32,0},{64,96},{96,64},{128,160},{160,128},{192,224},{224,1... | collective-permute-start | bytes 7688 | tf_op jit(solution)/shard_map/ppermute | solution.py:309
  59.3 4.3 %collective-permute-start.21 = (f32[5,128]{1,0:T(8,128)S(1)}, f32[5,128]{1,0:T(8,128)S(1)}, u32[]{:S(2)}, u32[]{:S(2)}) collective-permute-start(f32[5,128]{1,0:T(8,128)S(1)} %coarse_2.1.field), channel_id=1, source_target_pairs={{0,96},{32,64},{64,32},{96,0},{128,224},{160,192},{192,160},{224,1... | collective-permute-start | bytes 7688 | tf_op jit(solution)/shard_map/ppermute | solution.py:309
  60.6 3.4 %collective-permute-start.22 = (f32[5,128]{1,0:T(8,128)S(1)}, f32[5,128]{1,0:T(8,128)S(1)}, u32[]{:S(2)}, u32[]{:S(2)}) collective-permute-start(f32[5,128]{1,0:T(8,128)S(1)} %coarse_2.1.field), channel_id=1, source_target_pairs={{0,64},{32,96},{64,0},{96,32},{128,192},{160,224},{192,128},{224,1... | collective-permute-start | bytes 7688 | tf_op jit(solution)/shard_map/ppermute | solution.py:309
  64.2 9.7 %collective-permute-start.24 = (f32[5,4,128]{2,1,0:T(4,128)S(1)}, f32[5,4,128]{2,1,0:T(4,128)S(1)}, u32[]{:S(2)}, u32[]{:S(2)}) collective-permute-start(f32[5,4,128]{2,1,0:T(4,128)S(1)} %coarse_3.1.e), channel_id=1, source_target_pairs={{0,31},{1,0},{2,1},{3,2},{4,3},{5,4},{6,5},{7,6},{8,7},{9,8},{10,9... | collective-permute-start | bytes 30728 | tf_op jit(solution)/shard_map/ppermute | solution.py:305
  75.3 5.8 %collective-permute-start.27 = (f32[5,4,128]{2,1,0:T(4,128)S(1)}, f32[5,4,128]{2,1,0:T(4,128)S(1)}, u32[]{:S(2)}, u32[]{:S(2)}) collective-permute-start(f32[5,4,128]{2,1,0:T(4,128)S(1)} %middle_3.1.e), channel_id=1, source_target_pairs={{0,31},{1,0},{2,1},{3,2},{4,3},{5,4},{6,5},{7,6},{8,7},{9,8},{10,9... | collective-permute-start | bytes 30728 | tf_op jit(solution)/shard_map/ppermute | solution.py:305
  82.9 8.0 %collective-permute-start.30 = (f32[5,128]{1,0:T(8,128)S(1)}, f32[5,128]{1,0:T(8,128)S(1)}, u32[]{:S(2)}, u32[]{:S(2)}) collective-permute-start(f32[5,128]{1,0:T(8,128)S(1)} %get-tuple-element.68), channel_id=1, source_target_pairs={{0,30},{1,31},{2,0},{3,1},{4,2},{5,3},{6,4},{7,5},{8,6},{9,7},{10,... | collective-permute-start | bytes 7688 | tf_op jit(solution)/shard_map/ppermute | solution.py:305
  90.8 5.8 %collective-permute-start.33 = (f32[5,128]{1,0:T(8,128)S(1)}, f32[5,128]{1,0:T(8,128)S(1)}, u32[]{:S(2)}, u32[]{:S(2)}) collective-permute-start(f32[5,128]{1,0:T(8,128)S(1)} %get-tuple-element.71), channel_id=1, source_target_pairs={{0,2},{1,3},{2,4},{3,5},{4,6},{5,7},{6,8},{7,9},{8,10},{9,11},{10,... | collective-permute-start | bytes 7688 | tf_op jit(solution)/shard_map/ppermute | solution.py:305
  98.1 3.3 %collective-permute-start.34 = (f32[5,128]{1,0:T(8,128)S(1)}, f32[5,128]{1,0:T(8,128)S(1)}, u32[]{:S(2)}, u32[]{:S(2)}) collective-permute-start(f32[5,128]{1,0:T(8,128)S(1)} %get-tuple-element.73), channel_id=1, source_target_pairs={{0,30},{1,31},{2,0},{3,1},{4,2},{5,3},{6,4},{7,5},{8,6},{9,7},{10,... | collective-permute-start | bytes 7688 | tf_op jit(solution)/shard_map/ppermute | solution.py:305
  98.2 3.1 %collective-permute-start.35 = (f32[5,128]{1,0:T(8,128)S(1)}, f32[5,128]{1,0:T(8,128)S(1)}, u32[]{:S(2)}, u32[]{:S(2)}) collective-permute-start(f32[5,128]{1,0:T(8,128)S(1)} %get-tuple-element.74), channel_id=1, source_target_pairs={{0,31},{1,0},{2,1},{3,2},{4,3},{5,4},{6,5},{7,6},{8,7},{9,8},{10,9... | collective-permute-start | bytes 7688 | tf_op jit(solution)/shard_map/ppermute | solution.py:305
  100.0 5.8 %collective-permute-start.37 = (f32[5,128]{1,0:T(8,128)S(1)}, f32[5,128]{1,0:T(8,128)S(1)}, u32[]{:S(2)}, u32[]{:S(2)}) collective-permute-start(f32[5,128]{1,0:T(8,128)S(1)} %get-tuple-element.76), channel_id=1, source_target_pairs={{0,2},{1,3},{2,4},{3,5},{4,6},{5,7},{6,8},{7,9},{8,10},{9,11},{10,... | collective-permute-start | bytes 7688 | tf_op jit(solution)/shard_map/ppermute | solution.py:305
  (24 other events, 233.3 us)

commit v3 on v2

--- a/solution.py
+++ b/solution.py
@@ -175,7 +175,7 @@
 
 
 def down_kernel(
-    x, b, diag, coupling, columns, aggregate, m_inverse, r3, r2, r1, r0, rhs, e, residual
+    x, b, diag, coupling, columns, aggregate, m_inverse, r1, r0, r3, r2, rhs, e, residual
 ):
     table = fine_table(x, (r3, r2, r1, r0))
     for rows in HALVES:
@@ -329,8 +329,8 @@
     mid = (5, ROWS_MID // LANES, LANES)
     coarse = (5, ROWS_COARSE)
 
-    def fine_exchange(sends):
-        return [passed_along(sends[3 - j], -OFFSETS[j]) for j in (3, 2, 1, 0)]
+    def fine_exchange(sends, blocks=(3, 2, 1, 0)):
+        return [passed_along(sends[3 - j], -OFFSETS[j]) for j in blocks]
 
     def middle_exchange(e):
         right = passed_along(e, -1)
@@ -375,7 +375,7 @@
     rhs, e = call(
         "down",
         down_kernel,
-        (x, b, f_mats[0], f_mats[2], f_mats[3], f_aggregate, m_mats[1], *fine_exchange(sends)),
+        (x, b, f_mats[0], f_mats[2], f_mats[3], f_aggregate, m_mats[1], *fine_exchange(sends, (1, 0, 3, 2))),
         [mid, mid],
         [fine],
     )

time: 108 us -> 103 us (0.954)
  starting transfers between devices: 62.6 us -> 56.3 us
  waiting for transfers between devices: 32.6 us -> 33.9 us
    ppermute x28, starting transfers between devices: 47.7 us -> 41.3 us  [passed_along(): return lax.ppermute(x, 'dom', [(i, (i + by) % size) for i in range(size)])]
    ppermute x10, waiting for transfers between devices: 6.2 us -> 7.67 us  [group_swap(): lax.ppermute(x, 'grp', [(i, i ^ mask) for i in range(lax.axis_size('grp'))])]
where the time goes in v3:
time: 103 us
  starting transfers between devices  56.3 us (55%)
  waiting for transfers between devices  33.9 us (33%)
  Pallas kernels  12.2 us (12%)
    ppermute x28, starting transfers between devices, passed_along(): return lax.ppermute(x, 'dom', [(i, (i + by) % size) for i in range(size)])  41.3 us
    ppermute x28, waiting for transfers between devices, passed_along(): return lax.ppermute(x, 'dom', [(i, (i + by) % size) for i in range(size)])  26.2 us
    ppermute x10, starting transfers between devices, group_swap(): lax.ppermute(x, 'grp', [(i, i ^ mask) for i in range(lax.axis_size('grp'))])  15 us
    pallas_call x11, Pallas kernels, call(): pl.pallas_call(kernel, name=name, out_shape=[jax.ShapeDtypeStruct(s, F32)...  10.5 us
    ppermute x10, waiting for transfers between devices, group_swap(): lax.ppermute(x, 'grp', [(i, i ^ mask) for i in range(lax.axis_size('grp'))])  7.67 us
  transfers between devices with their start and end apart: 38, of which 19 were waited for; matrix products, arithmetic and copies ran while one was open for 0% of the time, Pallas kernels for 0%

profile of v3, /device:TPU:1, one launch (start us, length us, event | category | flops | bytes accessed | tf_op | source)
XLA Modules:
  0.0 102.7 jit_solution(4016385066545610879)
XLA Ops:
  0.0 1.7 %send.1 = (f32[5,128]{1,0:T(8,128)S(1)}, f32[5,128]{1,0:T(8,128)S(1)}, f32[5,128]{1,0:T(8,128)S(1)}, f32[5,128]{1,0:T(8,128)S(1)}, s32[4,128]{1,0:T(4,128)S(1)},...) custom-call(s32[4,64]{1,0:T(4,128)} %bitcast.63, ...), custom_call_target="tpu_custom_call" | custom-call | tf_op jit(solution)/shard_map/send/pallas_call | solution.py:347
  1.7 5.8 %collective-permute-start = (f32[5,128]{1,0:T(8,128)S(1)}, f32[5,128]{1,0:T(8,128)S(1)}, u32[]{:S(2)}, u32[]{:S(2)}) collective-permute-start(f32[5,128]{1,0:T(8,128)S(1)} %get-tuple-element.49), channel_id=1, source_target_pairs={{0,30},{1,31},{2,0},{3,1},{4,2},{5,3},{6,4},{7,5},{8,6},{9,7},{10,... | collective-permute-start | bytes 7688 | tf_op jit(solution)/shard_map/ppermute | solution.py:305
  10.5 4.5 %collective-permute-done.3.r0 = f32[5,128]{1,0:T(8,128)S(1)} collective-permute-done((f32[5,128]{1,0:T(8,128)S(1)}, f32[5,128]{1,0:T(8,128)S(1)}, u32[]{:S(2)}, u32[]{:S(2)}) %collective-permute-start.3) | collective-permute-done | bytes 2592 | tf_op jit(solution)/shard_map/ppermute | solution.py:305
  20.7 4.2 %collective-permute-done.7.r0 = f32[5,128]{1,0:T(8,128)S(1)} collective-permute-done((f32[5,128]{1,0:T(8,128)S(1)}, f32[5,128]{1,0:T(8,128)S(1)}, u32[]{:S(2)}, u32[]{:S(2)}) %collective-permute-start.7) | collective-permute-done | bytes 2592 | tf_op jit(solution)/shard_map/ppermute | solution.py:305
  26.8 1.6 %collective-permute-start.8 = (f32[5,128]{1,0:T(8,128)S(1)}, f32[5,128]{1,0:T(8,128)S(1)}, u32[]{:S(2)}, u32[]{:S(2)}) collective-permute-start(f32[5,128]{1,0:T(8,128)S(1)} %get-tuple-element.59), channel_id=1, source_target_pairs={{0,1},{1,2},{2,3},{3,4},{4,5},{5,6},{6,7},{7,8},{8,9},{9,10},{10,1... | collective-permute-start | bytes 7688 | tf_op jit(solution)/shard_map/ppermute | solution.py:305
  29.9 4.3 %collective-permute-done.9.r0 = f32[5,128]{1,0:T(8,128)S(1)} collective-permute-done((f32[5,128]{1,0:T(8,128)S(1)}, f32[5,128]{1,0:T(8,128)S(1)}, u32[]{:S(2)}, u32[]{:S(2)}) %collective-permute-start.9) | collective-permute-done | bytes 2592 | tf_op jit(solution)/shard_map/ppermute | solution.py:305
  34.2 1.6 %down.1 = (f32[5,4,128]{2,1,0:T(4,128)S(1)}, f32[5,4,128]{2,1,0:T(4,128)S(1)}) custom-call(f32[5,16,128]{2,1,0:T(8,128)S(1)} %get-tuple-element.58.x, f32[5,16,128]{2,1,0:T(8,128)S(1)} %get-tuple-element.42.b, f32[5,5,16,128]{3,2,1,0:T(8,128)S(1)} %get-tuple-element.43.diag, f32[6,5,5,16,128]{4,3,2,1,0:T(8,128)S(1)} %get-tuple-element.45.coupling, ...), custom_call_target="tpu_custom_call" | custom-call | tf_op jit(solution)/shard_map/down/pallas_call | solution.py:292
  35.9 1.7 %collective-permute-start.13 = (f32[5,4,128]{2,1,0:T(4,128)S(1)}, f32[5,4,128]{2,1,0:T(4,128)S(1)}, u32[]{:S(2)}, u32[]{:S(2)}) collective-permute-start(f32[5,4,128]{2,1,0:T(4,128)S(1)} %get-tuple-element.63.e), channel_id=1, source_target_pairs={{0,1},{1,2},{2,3},{3,4},{4,5},{5,6},{6,7},{7,8},{8,9},{9,10},{10,1... | collective-permute-start | bytes 30728 | tf_op jit(solution)/shard_map/ppermute | solution.py:305
  37.7 1.6 %collective-permute-start.14 = (f32[5,4,128]{2,1,0:T(4,128)S(1)}, f32[5,4,128]{2,1,0:T(4,128)S(1)}, u32[]{:S(2)}, u32[]{:S(2)}) collective-permute-start(f32[5,4,128]{2,1,0:T(4,128)S(1)} %get-tuple-element.63.e), channel_id=1, source_target_pairs={{0,32},{32,0},{64,96},{96,64},{128,160},{160,128},{192,224},{224,1... | collective-permute-start | bytes 30728 | tf_op jit(solution)/shard_map/ppermute | solution.py:309
  41.1 2.1 %collective-permute-start.15 = (f32[5,4,128]{2,1,0:T(4,128)S(1)}, f32[5,4,128]{2,1,0:T(4,128)S(1)}, u32[]{:S(2)}, u32[]{:S(2)}) collective-permute-start(f32[5,4,128]{2,1,0:T(4,128)S(1)} %middle_2.1.e), channel_id=1, source_target_pairs={{0,31},{1,0},{2,1},{3,2},{4,3},{5,4},{6,5},{7,6},{8,7},{9,8},{10,9... | collective-permute-start | bytes 30728 | tf_op jit(solution)/shard_map/ppermute | solution.py:305
  43.2 1.6 %collective-permute-start.17 = (f32[5,4,128]{2,1,0:T(4,128)S(1)}, f32[5,4,128]{2,1,0:T(4,128)S(1)}, u32[]{:S(2)}, u32[]{:S(2)}) collective-permute-start(f32[5,4,128]{2,1,0:T(4,128)S(1)} %middle_2.1.e), channel_id=1, source_target_pairs={{0,32},{32,0},{64,96},{96,64},{128,160},{160,128},{192,224},{224,1... | collective-permute-start | bytes 30728 | tf_op jit(solution)/shard_map/ppermute | solution.py:309
  46.4 4.3 %collective-permute-start.18 = (f32[5,128]{1,0:T(8,128)S(1)}, f32[5,128]{1,0:T(8,128)S(1)}, u32[]{:S(2)}, u32[]{:S(2)}) collective-permute-start(f32[5,128]{1,0:T(8,128)S(1)} %get-tuple-element.65.field), channel_id=1, source_target_pairs={{0,96},{32,64},{64,32},{96,0},{128,224},{160,192},{192,160},{224,1... | collective-permute-start | bytes 7688 | tf_op jit(solution)/shard_map/ppermute | solution.py:309
  51.7 2.4 %collective-permute-done.19.p2 = f32[5,128]{1,0:T(8,128)S(1)} collective-permute-done((f32[5,128]{1,0:T(8,128)S(1)}, f32[5,128]{1,0:T(8,128)S(1)}, u32[]{:S(2)}, u32[]{:S(2)}) %collective-permute-start.19) | collective-permute-done | bytes 2592 | tf_op jit(solution)/shard_map/ppermute | solution.py:309
  55.9 2.0 %collective-permute-start.23 = (f32[5,128]{1,0:T(8,128)S(1)}, f32[5,128]{1,0:T(8,128)S(1)}, u32[]{:S(2)}, u32[]{:S(2)}) collective-permute-start(f32[5,128]{1,0:T(8,128)S(1)} %coarse_2.1.field), channel_id=1, source_target_pairs={{0,32},{32,0},{64,96},{96,64},{128,160},{160,128},{192,224},{224,1... | collective-permute-start | bytes 7688 | tf_op jit(solution)/shard_map/ppermute | solution.py:309
  59.1 8.0 %collective-permute-start.24 = (f32[5,4,128]{2,1,0:T(4,128)S(1)}, f32[5,4,128]{2,1,0:T(4,128)S(1)}, u32[]{:S(2)}, u32[]{:S(2)}) collective-permute-start(f32[5,4,128]{2,1,0:T(4,128)S(1)} %coarse_3.1.e), channel_id=1, source_target_pairs={{0,31},{1,0},{2,1},{3,2},{4,3},{5,4},{6,5},{7,6},{8,7},{9,8},{10,9... | collective-permute-start | bytes 30728 | tf_op jit(solution)/shard_map/ppermute | solution.py:305
  67.1 1.7 %collective-permute-start.26 = (f32[5,4,128]{2,1,0:T(4,128)S(1)}, f32[5,4,128]{2,1,0:T(4,128)S(1)}, u32[]{:S(2)}, u32[]{:S(2)}) collective-permute-start(f32[5,4,128]{2,1,0:T(4,128)S(1)} %coarse_3.1.e), channel_id=1, source_target_pairs={{0,32},{32,0},{64,96},{96,64},{128,160},{160,128},{192,224},{224,1... | collective-permute-start | bytes 30728 | tf_op jit(solution)/shard_map/ppermute | solution.py:309
  70.3 4.0 %collective-permute-start.27 = (f32[5,4,128]{2,1,0:T(4,128)S(1)}, f32[5,4,128]{2,1,0:T(4,128)S(1)}, u32[]{:S(2)}, u32[]{:S(2)}) collective-permute-start(f32[5,4,128]{2,1,0:T(4,128)S(1)} %middle_3.1.e), channel_id=1, source_target_pairs={{0,31},{1,0},{2,1},{3,2},{4,3},{5,4},{6,5},{7,6},{8,7},{9,8},{10,9... | collective-permute-start | bytes 30728 | tf_op jit(solution)/shard_map/ppermute | solution.py:305
  74.3 1.7 %collective-permute-start.29 = (f32[5,4,128]{2,1,0:T(4,128)S(1)}, f32[5,4,128]{2,1,0:T(4,128)S(1)}, u32[]{:S(2)}, u32[]{:S(2)}) collective-permute-start(f32[5,4,128]{2,1,0:T(4,128)S(1)} %middle_3.1.e), channel_id=1, source_target_pairs={{0,32},{32,0},{64,96},{96,64},{128,160},{160,128},{192,224},{224,1... | collective-permute-start | bytes 30728 | tf_op jit(solution)/shard_map/ppermute | solution.py:309
  77.8 6.2 %collective-permute-start.30 = (f32[5,128]{1,0:T(8,128)S(1)}, f32[5,128]{1,0:T(8,128)S(1)}, u32[]{:S(2)}, u32[]{:S(2)}) collective-permute-start(f32[5,128]{1,0:T(8,128)S(1)} %get-tuple-element.68), channel_id=1, source_target_pairs={{0,30},{1,31},{2,0},{3,1},{4,2},{5,3},{6,4},{7,5},{8,6},{9,7},{10,... | collective-permute-start | bytes 7688 | tf_op jit(solution)/shard_map/ppermute | solution.py:305
  84.0 1.7 %collective-permute-start.32 = (f32[5,128]{1,0:T(8,128)S(1)}, f32[5,128]{1,0:T(8,128)S(1)}, u32[]{:S(2)}, u32[]{:S(2)}) collective-permute-start(f32[5,128]{1,0:T(8,128)S(1)} %get-tuple-element.70), channel_id=1, source_target_pairs={{0,1},{1,2},{2,3},{3,4},{4,5},{5,6},{6,7},{7,8},{8,9},{9,10},{10,1... | collective-permute-start | bytes 7688 | tf_op jit(solution)/shard_map/ppermute | solution.py:305
  87.1 4.5 %collective-permute-done.33.r0 = f32[5,128]{1,0:T(8,128)S(1)} collective-permute-done((f32[5,128]{1,0:T(8,128)S(1)}, f32[5,128]{1,0:T(8,128)S(1)}, u32[]{:S(2)}, u32[]{:S(2)}) %collective-permute-start.33) | collective-permute-done | bytes 2592 | tf_op jit(solution)/shard_map/ppermute | solution.py:305
  93.2 1.7 %collective-permute-start.36 = (f32[5,128]{1,0:T(8,128)S(1)}, f32[5,128]{1,0:T(8,128)S(1)}, u32[]{:S(2)}, u32[]{:S(2)}) collective-permute-start(f32[5,128]{1,0:T(8,128)S(1)} %get-tuple-element.75), channel_id=1, source_target_pairs={{0,1},{1,2},{2,3},{3,4},{4,5},{5,6},{6,7},{7,8},{8,9},{9,10},{10,1... | collective-permute-start | bytes 7688 | tf_op jit(solution)/shard_map/ppermute | solution.py:305
  96.3 4.4 %collective-permute-done.37.r0 = f32[5,128]{1,0:T(8,128)S(1)} collective-permute-done((f32[5,128]{1,0:T(8,128)S(1)}, f32[5,128]{1,0:T(8,128)S(1)}, u32[]{:S(2)}, u32[]{:S(2)}) %collective-permute-start.37) | collective-permute-done | bytes 2592 | tf_op jit(solution)/shard_map/ppermute | solution.py:305
  100.7 2.0 %fine_5.1 = f32[5,16,128]{2,1,0:T(8,128)} custom-call(f32[5,16,128]{2,1,0:T(8,128)S(1)} %get-tuple-element.72.x, f32[5,16,128]{2,1,0:T(8,128)S(1)} %get-tuple-element.42.b, f32[5,5,16,128]{3,2,1,0:T(8,128)S(1)} %get-tuple-element.43.diag, f32[5,5,16,128]{3,2,1,0:T(8,128)S(1)} %get-tuple-element.44.inverse, ...), custom_call_target="tpu_custom_call" | custom-call | tf_op jit(solution)/shard_map/fine_5/pallas_call | solution.py:292
  (88 shorter events, 27.1 us)
Async XLA Ops:
  1.7 7.6 %collective-permute-start = (f32[5,128]{1,0:T(8,128)S(1)}, f32[5,128]{1,0:T(8,128)S(1)}, u32[]{:S(2)}, u32[]{:S(2)}) collective-permute-start(f32[5,128]{1,0:T(8,128)S(1)} %get-tuple-element.49), channel_id=1, source_target_pairs={{0,30},{1,31},{2,0},{3,1},{4,2},{5,3},{6,4},{7,5},{8,6},{9,7},{10,... | collective-permute-start | bytes 7688 | tf_op jit(solution)/shard_map/ppermute | solution.py:305
  9.3 5.8 %collective-permute-start.3 = (f32[5,128]{1,0:T(8,128)S(1)}, f32[5,128]{1,0:T(8,128)S(1)}, u32[]{:S(2)}, u32[]{:S(2)}) collective-permute-start(f32[5,128]{1,0:T(8,128)S(1)} %get-tuple-element.52), channel_id=1, source_target_pairs={{0,2},{1,3},{2,4},{3,5},{4,6},{5,7},{6,8},{7,9},{8,10},{9,11},{10,... | collective-permute-start | bytes 7688 | tf_op jit(solution)/shard_map/ppermute | solution.py:305
  16.6 3.3 %collective-permute-start.4 = (f32[5,128]{1,0:T(8,128)S(1)}, f32[5,128]{1,0:T(8,128)S(1)}, u32[]{:S(2)}, u32[]{:S(2)}) collective-permute-start(f32[5,128]{1,0:T(8,128)S(1)} %get-tuple-element.54), channel_id=1, source_target_pairs={{0,30},{1,31},{2,0},{3,1},{4,2},{5,3},{6,4},{7,5},{8,6},{9,7},{10,... | collective-permute-start | bytes 7688 | tf_op jit(solution)/shard_map/ppermute | solution.py:305
  17.2 3.5 %collective-permute-start.5 = (f32[5,128]{1,0:T(8,128)S(1)}, f32[5,128]{1,0:T(8,128)S(1)}, u32[]{:S(2)}, u32[]{:S(2)}) collective-permute-start(f32[5,128]{1,0:T(8,128)S(1)} %get-tuple-element.55), channel_id=1, source_target_pairs={{0,31},{1,0},{2,1},{3,2},{4,3},{5,4},{6,5},{7,6},{8,7},{9,8},{10,9... | collective-permute-start | bytes 7688 | tf_op jit(solution)/shard_map/ppermute | solution.py:305
  19.1 5.8 %collective-permute-start.7 = (f32[5,128]{1,0:T(8,128)S(1)}, f32[5,128]{1,0:T(8,128)S(1)}, u32[]{:S(2)}, u32[]{:S(2)}) collective-permute-start(f32[5,128]{1,0:T(8,128)S(1)} %get-tuple-element.57), channel_id=1, source_target_pairs={{0,2},{1,3},{2,4},{3,5},{4,6},{5,7},{6,8},{7,9},{8,10},{9,11},{10,... | collective-permute-start | bytes 7688 | tf_op jit(solution)/shard_map/ppermute | solution.py:305
  26.5 3.3 %collective-permute-start.10 = (f32[5,128]{1,0:T(8,128)S(1)}, f32[5,128]{1,0:T(8,128)S(1)}, u32[]{:S(2)}, u32[]{:S(2)}) collective-permute-start(f32[5,128]{1,0:T(8,128)S(1)} %get-tuple-element.61), channel_id=1, source_target_pairs={{0,30},{1,31},{2,0},{3,1},{4,2},{5,3},{6,4},{7,5},{8,6},{9,7},{10,... | collective-permute-start | bytes 7688 | tf_op jit(solution)/shard_map/ppermute | solution.py:305
  26.6 3.3 %collective-permute-start.11 = (f32[5,128]{1,0:T(8,128)S(1)}, f32[5,128]{1,0:T(8,128)S(1)}, u32[]{:S(2)}, u32[]{:S(2)}) collective-permute-start(f32[5,128]{1,0:T(8,128)S(1)} %get-tuple-element.62), channel_id=1, source_target_pairs={{0,31},{1,0},{2,1},{3,2},{4,3},{5,4},{6,5},{7,6},{8,7},{9,8},{10,9... | collective-permute-start | bytes 7688 | tf_op jit(solution)/shard_map/ppermute | solution.py:305
  26.8 3.2 %collective-permute-start.8 = (f32[5,128]{1,0:T(8,128)S(1)}, f32[5,128]{1,0:T(8,128)S(1)}, u32[]{:S(2)}, u32[]{:S(2)}) collective-permute-start(f32[5,128]{1,0:T(8,128)S(1)} %get-tuple-element.59), channel_id=1, source_target_pairs={{0,1},{1,2},{2,3},{3,4},{4,5},{5,6},{6,7},{7,8},{8,9},{9,10},{10,1... | collective-permute-start | bytes 7688 | tf_op jit(solution)/shard_map/ppermute | solution.py:305
  28.4 5.8 %collective-permute-start.9 = (f32[5,128]{1,0:T(8,128)S(1)}, f32[5,128]{1,0:T(8,128)S(1)}, u32[]{:S(2)}, u32[]{:S(2)}) collective-permute-start(f32[5,128]{1,0:T(8,128)S(1)} %get-tuple-element.60), channel_id=1, source_target_pairs={{0,2},{1,3},{2,4},{3,5},{4,6},{5,7},{6,8},{7,9},{8,10},{9,11},{10,... | collective-permute-start | bytes 7688 | tf_op jit(solution)/shard_map/ppermute | solution.py:305
  35.8 3.5 %collective-permute-start.12 = (f32[5,4,128]{2,1,0:T(4,128)S(1)}, f32[5,4,128]{2,1,0:T(4,128)S(1)}, u32[]{:S(2)}, u32[]{:S(2)}) collective-permute-start(f32[5,4,128]{2,1,0:T(4,128)S(1)} %get-tuple-element.63.e), channel_id=1, source_target_pairs={{0,31},{1,0},{2,1},{3,2},{4,3},{5,4},{6,5},{7,6},{8,7},{9,8},{10,9... | collective-permute-start | bytes 30728 | tf_op jit(solution)/shard_map/ppermute | solution.py:305
  35.9 3.4 %collective-permute-start.13 = (f32[5,4,128]{2,1,0:T(4,128)S(1)}, f32[5,4,128]{2,1,0:T(4,128)S(1)}, u32[]{:S(2)}, u32[]{:S(2)}) collective-permute-start(f32[5,4,128]{2,1,0:T(4,128)S(1)} %get-tuple-element.63.e), channel_id=1, source_target_pairs={{0,1},{1,2},{2,3},{3,4},{4,5},{5,6},{6,7},{7,8},{8,9},{9,10},{10,1... | collective-permute-start | bytes 30728 | tf_op jit(solution)/shard_map/ppermute | solution.py:305
  41.1 3.7 %collective-permute-start.15 = (f32[5,4,128]{2,1,0:T(4,128)S(1)}, f32[5,4,128]{2,1,0:T(4,128)S(1)}, u32[]{:S(2)}, u32[]{:S(2)}) collective-permute-start(f32[5,4,128]{2,1,0:T(4,128)S(1)} %middle_2.1.e), channel_id=1, source_target_pairs={{0,31},{1,0},{2,1},{3,2},{4,3},{5,4},{6,5},{7,6},{8,7},{9,8},{10,9... | collective-permute-start | bytes 30728 | tf_op jit(solution)/shard_map/ppermute | solution.py:305
  46.4 5.2 %collective-permute-start.18 = (f32[5,128]{1,0:T(8,128)S(1)}, f32[5,128]{1,0:T(8,128)S(1)}, u32[]{:S(2)}, u32[]{:S(2)}) collective-permute-start(f32[5,128]{1,0:T(8,128)S(1)} %get-tuple-element.65.field), channel_id=1, source_target_pairs={{0,96},{32,64},{64,32},{96,0},{128,224},{160,192},{192,160},{224,1... | collective-permute-start | bytes 7688 | tf_op jit(solution)/shard_map/ppermute | solution.py:309
  50.7 3.4 %collective-permute-start.19 = (f32[5,128]{1,0:T(8,128)S(1)}, f32[5,128]{1,0:T(8,128)S(1)}, u32[]{:S(2)}, u32[]{:S(2)}) collective-permute-start(f32[5,128]{1,0:T(8,128)S(1)} %get-tuple-element.65.field), channel_id=1, source_target_pairs={{0,64},{32,96},{64,0},{96,32},{128,192},{160,224},{192,128},{224,1... | collective-permute-start | bytes 7688 | tf_op jit(solution)/shard_map/ppermute | solution.py:309
  50.7 3.4 %collective-permute-start.20 = (f32[5,128]{1,0:T(8,128)S(1)}, f32[5,128]{1,0:T(8,128)S(1)}, u32[]{:S(2)}, u32[]{:S(2)}) collective-permute-start(f32[5,128]{1,0:T(8,128)S(1)} %get-tuple-element.65.field), channel_id=1, source_target_pairs={{0,32},{32,0},{64,96},{96,64},{128,160},{160,128},{192,224},{224,1... | collective-permute-start | bytes 7688 | tf_op jit(solution)/shard_map/ppermute | solution.py:309
  54.2 4.3 %collective-permute-start.21 = (f32[5,128]{1,0:T(8,128)S(1)}, f32[5,128]{1,0:T(8,128)S(1)}, u32[]{:S(2)}, u32[]{:S(2)}) collective-permute-start(f32[5,128]{1,0:T(8,128)S(1)} %coarse_2.1.field), channel_id=1, source_target_pairs={{0,96},{32,64},{64,32},{96,0},{128,224},{160,192},{192,160},{224,1... | collective-permute-start | bytes 7688 | tf_op jit(solution)/shard_map/ppermute | solution.py:309
  55.5 3.4 %collective-permute-start.22 = (f32[5,128]{1,0:T(8,128)S(1)}, f32[5,128]{1,0:T(8,128)S(1)}, u32[]{:S(2)}, u32[]{:S(2)}) collective-permute-start(f32[5,128]{1,0:T(8,128)S(1)} %coarse_2.1.field), channel_id=1, source_target_pairs={{0,64},{32,96},{64,0},{96,32},{128,192},{160,224},{192,128},{224,1... | collective-permute-start | bytes 7688 | tf_op jit(solution)/shard_map/ppermute | solution.py:309
  59.1 9.7 %collective-permute-start.24 = (f32[5,4,128]{2,1,0:T(4,128)S(1)}, f32[5,4,128]{2,1,0:T(4,128)S(1)}, u32[]{:S(2)}, u32[]{:S(2)}) collective-permute-start(f32[5,4,128]{2,1,0:T(4,128)S(1)} %coarse_3.1.e), channel_id=1, source_target_pairs={{0,31},{1,0},{2,1},{3,2},{4,3},{5,4},{6,5},{7,6},{8,7},{9,8},{10,9... | collective-permute-start | bytes 30728 | tf_op jit(solution)/shard_map/ppermute | solution.py:305
  70.3 5.8 %collective-permute-start.27 = (f32[5,4,128]{2,1,0:T(4,128)S(1)}, f32[5,4,128]{2,1,0:T(4,128)S(1)}, u32[]{:S(2)}, u32[]{:S(2)}) collective-permute-start(f32[5,4,128]{2,1,0:T(4,128)S(1)} %middle_3.1.e), channel_id=1, source_target_pairs={{0,31},{1,0},{2,1},{3,2},{4,3},{5,4},{6,5},{7,6},{8,7},{9,8},{10,9... | collective-permute-start | bytes 30728 | tf_op jit(solution)/shard_map/ppermute | solution.py:305
  77.8 8.0 %collective-permute-start.30 = (f32[5,128]{1,0:T(8,128)S(1)}, f32[5,128]{1,0:T(8,128)S(1)}, u32[]{:S(2)}, u32[]{:S(2)}) collective-permute-start(f32[5,128]{1,0:T(8,128)S(1)} %get-tuple-element.68), channel_id=1, source_target_pairs={{0,30},{1,31},{2,0},{3,1},{4,2},{5,3},{6,4},{7,5},{8,6},{9,7},{10,... | collective-permute-start | bytes 7688 | tf_op jit(solution)/shard_map/ppermute | solution.py:305
  85.8 5.8 %collective-permute-start.33 = (f32[5,128]{1,0:T(8,128)S(1)}, f32[5,128]{1,0:T(8,128)S(1)}, u32[]{:S(2)}, u32[]{:S(2)}) collective-permute-start(f32[5,128]{1,0:T(8,128)S(1)} %get-tuple-element.71), channel_id=1, source_target_pairs={{0,2},{1,3},{2,4},{3,5},{4,6},{5,7},{6,8},{7,9},{8,10},{9,11},{10,... | collective-permute-start | bytes 7688 | tf_op jit(solution)/shard_map/ppermute | solution.py:305
  93.0 3.3 %collective-permute-start.34 = (f32[5,128]{1,0:T(8,128)S(1)}, f32[5,128]{1,0:T(8,128)S(1)}, u32[]{:S(2)}, u32[]{:S(2)}) collective-permute-start(f32[5,128]{1,0:T(8,128)S(1)} %get-tuple-element.73), channel_id=1, source_target_pairs={{0,30},{1,31},{2,0},{3,1},{4,2},{5,3},{6,4},{7,5},{8,6},{9,7},{10,... | collective-permute-start | bytes 7688 | tf_op jit(solution)/shard_map/ppermute | solution.py:305
  93.2 3.1 %collective-permute-start.35 = (f32[5,128]{1,0:T(8,128)S(1)}, f32[5,128]{1,0:T(8,128)S(1)}, u32[]{:S(2)}, u32[]{:S(2)}) collective-permute-start(f32[5,128]{1,0:T(8,128)S(1)} %get-tuple-element.74), channel_id=1, source_target_pairs={{0,31},{1,0},{2,1},{3,2},{4,3},{5,4},{6,5},{7,6},{8,7},{9,8},{10,9... | collective-permute-start | bytes 7688 | tf_op jit(solution)/shard_map/ppermute | solution.py:305
  95.0 5.8 %collective-permute-start.37 = (f32[5,128]{1,0:T(8,128)S(1)}, f32[5,128]{1,0:T(8,128)S(1)}, u32[]{:S(2)}, u32[]{:S(2)}) collective-permute-start(f32[5,128]{1,0:T(8,128)S(1)} %get-tuple-element.76), channel_id=1, source_target_pairs={{0,2},{1,3},{2,4},{3,5},{4,6},{5,7},{6,8},{7,9},{8,10},{9,11},{10,... | collective-permute-start | bytes 7688 | tf_op jit(solution)/shard_map/ppermute | solution.py:305
  (24 other events, 204.1 us)
